TPU v7x, 32 devices: a whole 2x2x4 slice. The times are simulated.
32 devices in a mesh: gx: 2 (over x), gy: 4 (over y, core), gz: 4 (over z).
Axes of the slice: x: 2, y: 2, z: 4, core: 2. Of those that a mesh axis runs over, the one named last changes fastest.
Arguments:
- tokens: bfloat16 [8192, 768], P(('gx', 'gy', 'gz')), may hold values from -6 to 6
- norm_gain: float32 [768], replicated, may hold values from 0.5 to 1.5
- w_qkv: bfloat16 [768, 2304], replicated
- w_out: bfloat16 [768, 768], replicated, may hold values from -0.21875 to 0.21875
- send_rows: int32 [32, 7, 32], P(('gx', 'gy', 'gz')), may hold values from -1 to 255, as said below
- window_rows: int32 [32, 512], P(('gx', 'gy', 'gz')), may hold values from -1 to 479, as said below
- grad_out: bfloat16 [8192, 768], P(('gx', 'gy', 'gz')), may hold values from -6 to 6
Outputs:
- block_out: bfloat16 [8192, 768], P(('gx', 'gy', 'gz'))
- grad_tokens: bfloat16 [8192, 768], P(('gx', 'gy', 'gz'))
- grad_gain: float32 [768], P(('gx', 'gy', 'gz'))
- grad_w_qkv: float32 [768, 2304], P(('gx', 'gy', 'gz'))
- grad_w_out: float32 [768, 768], P(('gx', 'gy', 'gz'))
Inputs may be any that keep to these rules, and one draw needn't show every extreme that they name: `send_rows`: entries are rows of the tile (0 to 255) or -1 for empty; in each list the rows come first; a row stands in at most one list of its tile; a tile at the upper end of an axis has no rows in lists toward that axis; tile 0 fills all 7 lists. `window_rows`: entries index the owner's row list (256 own rows, then the 7 received lists of 32 in order k) or are -1 for padding; every own row that no list sends away and every non-empty received entry fills exactly one slot, nothing else does; a device's filled slots make whole windows but one.
All inputs are finite; a program needn't handle non-finite values.
Results may differ from a plain program's by a relative error of at most 0.018.
Values may be sent and summed in bfloat16 or wider, within the bound.
A program may use at most 128 MiB of HBM per device.

v0:
```python
import jax
import jax.numpy as jnp
from jax import lax
from jax.sharding import PartitionSpec as P

HEADS = 12
WCAP = 128


epsilon = 1e-06
big_negative = -1e30


def passed_along(value, axis, steps):
    count = lax.axis_size(axis)
    initial, last = (max(0, -steps), min(count, count - steps))
    return lax.ppermute(value, axis, [(source, source + steps) for source in range(initial, last)])


def gather_rows(table, index):
    safe = jnp.maximum(index, 0)
    taken = jnp.take(table, safe, axis=0)
    return jnp.where((index >= 0)[..., None], taken, jnp.zeros((), table.dtype))


def spread_rows(values, index, length):
    target = jnp.where(index >= 0, index, length)
    empty = jnp.zeros((length, values.shape[-1]), values.dtype)
    return empty.at[target].set(values, mode="drop")


def carry_up(blocks):
    from_x = passed_along(blocks[3:7], "gx", 1)
    section_y = jnp.stack([blocks[1], blocks[2], from_x[2], from_x[3]])
    from_y = passed_along(section_y, "gy", 1)
    section_z = jnp.stack([blocks[0], from_y[1], from_x[1], from_y[3]])
    from_z = passed_along(section_z, "gz", 1)
    return jnp.concatenate(
        [from_z[0], from_y[0], from_z[1], from_x[0], from_z[2], from_y[2], from_z[3]], axis=0
    )


def carry_down(arrived, send, count):
    width = arrived.shape[-1]
    parts = arrived.reshape(7, send.shape[1], width)
    down_z = passed_along(jnp.stack([parts[0], parts[2], parts[4], parts[6]]), "gz", -1)
    down_y = passed_along(jnp.stack([parts[1], down_z[1], parts[5], down_z[3]]), "gy", -1)
    down_x = passed_along(jnp.stack([parts[3], down_z[2], down_y[2], down_y[3]]), "gx", -1)
    returned = jnp.stack(
        [down_z[0], down_y[0], down_y[1], down_x[0], down_x[1], down_x[2], down_x[3]]
    )
    return spread_rows(returned.reshape(-1, width), send.reshape(-1), count)


def split_heads(packed, heads):
    windows, length, triple = packed.shape
    head_dim = triple // 3 // heads
    split = packed.reshape(windows, length, 3, heads, head_dim)
    return (split[:, :, 0], split[:, :, 1], split[:, :, 2], head_dim)


def attend(packed, valid, heads):
    query, keys, values, head_dim = split_heads(packed, heads)
    scores = jnp.einsum(
        "wqhd,wkhd->whqk", query, keys, preferred_element_type=jnp.float32
    ) * head_dim ** (-0.5)
    scores = jnp.where(valid[:, None, None, :], scores, big_negative)
    top = jnp.max(scores, axis=-1, keepdims=True)
    expo = jnp.exp(scores - top)
    probs = expo / jnp.sum(expo, axis=-1, keepdims=True)
    weights = probs.astype(jnp.bfloat16)
    mixed = jnp.einsum(
        "whqk,wkhd->wqhd", weights, values, preferred_element_type=jnp.float32
    ).astype(jnp.bfloat16)
    return (mixed.reshape(packed.shape[0] * packed.shape[1], -1), probs, weights)


def attend_back(packed, probs, weights, delta_slots, heads):
    query, keys, values, head_dim = split_heads(packed, heads)
    windows, length = (packed.shape[0], packed.shape[1])
    grad_delta = delta_slots.reshape(windows, length, heads, head_dim)
    dweights = jnp.einsum("wqhd,wkhd->whqk", grad_delta, values, preferred_element_type=jnp.float32)
    dscores = probs * (dweights - jnp.sum(dweights * probs, axis=-1, keepdims=True))
    dscaled = (dscores * head_dim ** (-0.5)).astype(jnp.bfloat16)
    dquery = jnp.einsum("whqk,wkhd->wqhd", dscaled, keys, preferred_element_type=jnp.float32)
    dkeys = jnp.einsum("whqk,wqhd->wkhd", dscaled, query, preferred_element_type=jnp.float32)
    dvalues = jnp.einsum("whqk,wqhd->wkhd", weights, grad_delta, preferred_element_type=jnp.float32)
    joined = jnp.stack([dquery, dkeys, dvalues], axis=2)
    return joined.reshape(windows * length, -1).astype(jnp.bfloat16)


def on_device(tokens, norm_gain, w_qkv, w_out, send_rows, window_rows, grad_out):
    count = tokens.shape[0]
    send = send_rows[0]
    slot_index = window_rows[0]
    windows = slot_index.shape[0] // WCAP
    valid = (slot_index >= 0).reshape(windows, WCAP)
    span = count + send.shape[0] * send.shape[1]
    floats = tokens.astype(jnp.float32)
    centred = floats - jnp.mean(floats, axis=-1, keepdims=True)
    inv_std = lax.rsqrt(jnp.mean(centred * centred, axis=-1, keepdims=True) + epsilon)
    unit = centred * inv_std
    normed = (unit * norm_gain).astype(jnp.bfloat16)
    delta_own = jnp.einsum("te,de->td", grad_out, w_out, preferred_element_type=jnp.float32).astype(
        jnp.bfloat16
    )
    source = jnp.dot(normed, w_qkv, preferred_element_type=jnp.float32).astype(jnp.bfloat16)
    source_in = carry_up(gather_rows(source, send))
    local = jnp.concatenate([source, source_in], axis=0)
    packed = gather_rows(local, slot_index).reshape(windows, WCAP, -1)
    mixed, probs, weights = attend(packed, valid, HEADS)
    mixed_rows = spread_rows(mixed, slot_index, span)
    attended = mixed_rows[:count] + carry_down(mixed_rows[count:], send, count)
    block_out = (floats + jnp.dot(attended, w_out, preferred_element_type=jnp.float32)).astype(
        jnp.bfloat16
    )
    grad_proj = jnp.einsum("td,te->de", attended, grad_out, preferred_element_type=jnp.float32)
    delta_in = carry_up(gather_rows(delta_own, send))
    delta_slots = gather_rows(jnp.concatenate([delta_own, delta_in], axis=0), slot_index)
    dpacked = attend_back(packed, probs, weights, delta_slots, HEADS)
    dpacked_rows = spread_rows(dpacked, slot_index, span)
    dpacked_own = dpacked_rows[:count] + carry_down(dpacked_rows[count:], send, count)
    grad_qkv = jnp.einsum("td,te->de", normed, dpacked_own, preferred_element_type=jnp.float32)
    dnormed = jnp.einsum(
        "te,de->td", dpacked_own, w_qkv, preferred_element_type=jnp.float32
    ).astype(jnp.bfloat16)
    dnormed_f = dnormed.astype(jnp.float32)
    grad_gain = jnp.sum(dnormed_f * unit, axis=0)
    dunit = dnormed_f * norm_gain
    dcentre = inv_std * (
        dunit
        - jnp.mean(dunit, axis=-1, keepdims=True)
        - unit * jnp.mean(dunit * unit, axis=-1, keepdims=True)
    )
    grad_tokens = (grad_out.astype(jnp.float32) + dcentre).astype(jnp.bfloat16)
    totals = (
        lax.psum_scatter(grad_gain, ("gx", "gy", "gz"), scatter_dimension=0, tiled=True),
        lax.psum_scatter(grad_qkv, ("gx", "gy", "gz"), scatter_dimension=0, tiled=True),
        lax.psum_scatter(grad_proj, ("gx", "gy", "gz"), scatter_dimension=0, tiled=True),
    )
    return (block_out, grad_tokens, totals[0], totals[1], totals[2])


def solution(mesh):
    in_specs = (
        P(("gx", "gy", "gz"), None),
        P(),
        P(),
        P(),
        P(("gx", "gy", "gz"), None, None),
        P(("gx", "gy", "gz"), None),
        P(("gx", "gy", "gz"), None),
    )
    out_specs = (
        P(("gx", "gy", "gz"), None),
        P(("gx", "gy", "gz"), None),
        P(("gx", "gy", "gz")),
        P(("gx", "gy", "gz"), None),
        P(("gx", "gy", "gz"), None),
    )
    return jax.shard_map(
        on_device, mesh=mesh, in_specs=in_specs, out_specs=out_specs, check_vma=False
    )
```

profile of v0, /device:TPU:0, one launch (start us, length us, event | category | flops | bytes accessed | tf_op | source)
XLA Modules:
  0.0 434.1 jit_solution(15841693450695796712)
XLA Ops:
  16.8 4.7 %gather_fusion = bf16[224,2304]{1,0:T(8,128)(2,1)} fusion(bf16[256,2304]{1,0:T(8,128)(2,1)} %get-tuple-element.47, s32[1024]{0:T(1024)S(1)} %pad_clamp_fusion.1), kind=kCustom, calls=%fused_computation | custom fusion | bytes 2065280 | tf_op jit(solution)/shard_map/jit(_take)/gather | solution.py:22
  25.7 5.7 %collective-permute-start = (bf16[4,32,2304]{2,1,0:T(8,128)(2,1)}, bf16[4,32,2304]{2,1,0:T(8,128)(2,1)}, u32[]{:S(2)}, u32[]{:S(2)}) collective-permute-start(bf16[4,32,2304]{2,1,0:T(8,128)(2,1)} %slice.347), channel_id=1, source_target_pairs={{0,16},{1,17},{2,18},{3,19},{4,20},{5,21},{6,22},{7,23},{8,24},{9,... | collective-permute-start | bytes 1769480 | tf_op jit(solution)/shard_map/ppermute | solution.py:17
  59.1 4.5 %collective-permute-start.1 = (bf16[4,32,2304]{2,1,0:T(8,128)(2,1)S(1)}, bf16[4,32,2304]{2,1,0:T(8,128)(2,1)S(1)}, u32[]{:S(2)}, u32[]{:S(2)}) collective-permute-start(bf16[4,32,2304]{2,1,0:T(8,128)(2,1)S(1)} %pad_maximum_fusion.2), channel_id=1, source_target_pairs={{0,4},{4,8},{8,12},{1,5},{5,9},{9,13},{2,6},{6,10},{10,14},{3,7},{... | collective-permute-start | bytes 1769480 | tf_op jit(solution)/shard_map/ppermute | solution.py:17
  70.2 4.8 %collective-permute-start.2 = (bf16[4,32,2304]{2,1,0:T(8,128)(2,1)}, bf16[4,32,2304]{2,1,0:T(8,128)(2,1)}, u32[]{:S(2)}, u32[]{:S(2)}) collective-permute-start(bf16[4,32,2304]{2,1,0:T(8,128)(2,1)} %pad_maximum_fusion.3), channel_id=1, source_target_pairs={{0,1},{1,2},{2,3},{4,5},{5,6},{6,7},{8,9},{9,10},{10,11},{12,13},{... | collective-permute-start | bytes 1769480 | tf_op jit(solution)/shard_map/ppermute | solution.py:17
  76.2 4.3 gather_fusion.3
  98.7 7.7 %gather_fusion.1 = bf16[512,2304]{1,0:T(8,128)(2,1)} fusion(bf16[480,2304]{1,0:T(8,128)(2,1)} %fusion.63, s32[1024]{0:T(1024)S(1)} %pad_clamp_fusion), kind=kCustom, calls=%fused_computation.1 | custom fusion | bytes 4720640 | tf_op jit(solution)/shard_map/jit(_take)/gather | solution.py:22
  106.3 4.3 copy.41
  110.6 5.3 %gather.22 = bf16[4,128,3,12,64]{1,0,4,3,2:T(4,128)(2,1)} reshape(bf16[512,2304]{0,1:T(8,128)(2,1)} %copy.41) | data formatting | bytes 4718592 | tf_op jit(solution)/shard_map/jit(_take)/gather | solution.py:22
  124.4 6.8 %fusion.27 = bf16[4,128,1,12,64]{1,4,3,0,2:T(8,128)(2,1)} fusion(f32[4,12,128,128]{2,3,1,0:T(8,128)} %fusion.52, bf16[4,128,3,12,64]{1,4,3,0,2:T(8,128)(2,1)} %copy-done.1, f32[4,12,128,128]{2,3,1,0:T(8,128)} %copy-done.21, f32[4,12,128]{2,1,0:T(8,128)} %copy-done.22), kind=kOutput, calls=%fused_computation.34 | convolution fusion | flops 106567808 | bytes 14221312 | tf_op jit(solution)/shard_map/whqk,wkhd->wqhd/dot_general | solution.py:85
  131.2 6.9 %fusion.24 = bf16[4,128,1,12,64]{1,4,3,0,2:T(8,128)(2,1)} fusion(f32[4,12,128,128]{2,3,1,0:T(8,128)} %fusion.52, bf16[4,128,3,12,64]{1,4,3,0,2:T(8,128)(2,1)} %copy-done.1, f32[4,12,128,128]{2,3,1,0:T(8,128)} %copy-done.21, f32[4,12,128]{2,1,0:T(8,128)} %copy-done.22), kind=kOutput, calls=%fused_computation.33 | convolution fusion | flops 106567808 | bytes 14221312 | tf_op jit(solution)/shard_map/whqk,wqhd->wkhd/dot_general | solution.py:86
  138.1 4.2 fusion.31
  146.3 4.2 scatter_custom_fusion
  160.0 4.5 %copy.53 = bf16[512,2304]{1,0:T(8,128)(2,1)} copy(bf16[512,2304]{0,1:T(8,128)(2,1)} %bitcast.151) | data formatting | bytes 4718592 | tf_op jit(solution)/shard_map/convert_element_type | solution.py:89
  164.5 6.6 %scatter_custom_fusion.2 = bf16[480,2304]{1,0:T(8,128)(2,1)} fusion(s32[512]{0:T(512)} %bitcast.165, bf16[512,2304]{1,0:T(8,128)(2,1)} %copy.53, bf16[]{:T(256)} %constant.44.clone.1), kind=kCustom, calls=%fused_computation.45 | custom fusion | bytes 2212352 | tf_op jit(solution)/shard_map/scatter | solution.py:29
  176.8 6.0 %collective-permute-done.4 = bf16[4,32,768]{2,1,0:T(8,128)(2,1)S(1)} collective-permute-done((bf16[4,32,768]{2,1,0:T(8,128)(2,1)S(1)}, bf16[4,32,768]{2,1,0:T(8,128)(2,1)S(1)}, u32[]{:S(2)}, u32[]{:S(2)}) %collective-permute-start.4) | collective-permute-done | bytes 196640 | tf_op jit(solution)/shard_map/ppermute | solution.py:17
  184.1 4.3 collective-permute-done.9
  199.7 6.5 %collective-permute-done.10 = bf16[4,32,2304]{2,1,0:T(8,128)(2,1)S(1)} collective-permute-done((bf16[4,32,2304]{2,1,0:T(8,128)(2,1)S(1)}, bf16[4,32,2304]{2,1,0:T(8,128)(2,1)S(1)}, u32[]{:S(2)}, u32[]{:S(2)}) %collective-permute-start.10) | collective-permute-done | bytes 589856 | tf_op jit(solution)/shard_map/ppermute | solution.py:17
  207.7 10.5 %collective-permute-done.11 = bf16[4,32,2304]{2,1,0:T(8,128)(2,1)S(1)} collective-permute-done((bf16[4,32,2304]{2,1,0:T(8,128)(2,1)S(1)}, bf16[4,32,2304]{2,1,0:T(8,128)(2,1)S(1)}, u32[]{:S(2)}, u32[]{:S(2)}) %collective-permute-start.11) | collective-permute-done | bytes 589856 | tf_op jit(solution)/shard_map/ppermute | solution.py:17
  219.2 4.1 scatter_custom_fusion.3
  223.4 6.0 %fusion.60 = f32[768,2304]{1,0:T(8,128)} fusion(bf16[256,2304]{1,0:T(8,128)(2,1)} %scatter_custom_fusion.3, bf16[480,2304]{1,0:T(8,128)(2,1)} %scatter_custom_fusion.2, bf16[256,768]{1,0:T(8,128)(2,1)} %param.7, f32[768]{0:T(1024)S(1)} %copy-done.16, f32[256]{0:T(256)S(1)} %add_rsqrt_fusion, f32[256]{0:T(256)S(1)} %broadcast_multiply_fusion.2), kind=kOutput, calls=%fused_computation.87 | convolution fusion | flops 907542528 | bytes 9835520 | tf_op jit(solution)/shard_map/td,te->de/dot_general | solution.py:123
  232.4 3.9 fusion.48
  236.3 47.2 %all-reduce = f32[768]{0:T(1024)} all-reduce(f32[768]{0:T(1024)S(1)} %get-tuple-element.5), channel_id=2, replica_groups=mesh['gx'=2,'gy'=4,'gz'=4] {'gx','gy','gz'}, use_global_device_ids=true, to_apply=%region_12.13.clone | all-reduce | flops 768 | bytes 6144
  288.5 13.1 %reduce-scatter.5.cloned.1.call-done = f32[24,768]{1,0:T(8,128)} async-done(((f32[768,768]{1,0:T(8,128)}), f32[24,768]{1,0:T(8,128)}) %reduce-scatter.5.cloned.1.call-update) | async-done | bytes 73744 | tf_op jit(solution)/shard_map/reduce_scatter | solution.py:139
  301.6 125.4 %reduce-scatter.3.cloned.1.call-done = f32[24,2304]{1,0:T(8,128)} async-done(((f32[768,2304]{1,0:T(8,128)}), f32[24,2304]{1,0:T(8,128)}) %reduce-scatter.3.cloned.1.call-update) | async-done | bytes 221200 | tf_op jit(solution)/shard_map/reduce_scatter | solution.py:138
  (152 shorter events, 117.9 us)
Async XLA Ops:
  7.2 294.4 %reduce-scatter.5.cloned.1.call-start = ((), (), s32[]{:S(2)}) async-start(), calls=%async_computation.3 | async-start | bytes 2433024 | tf_op jit(solution)/shard_map/reduce_scatter | solution.py:139
  21.6 9.8 %copy-start.5 = (bf16[256,768]{1,0:T(8,128)(2,1)S(1)}, bf16[256,768]{1,0:T(8,128)(2,1)}, u32[]{:S(2)}) copy-start(bf16[256,768]{1,0:T(8,128)(2,1)} %param.13) | copy-start | bytes 1179652
  21.6 9.8 %copy-start.7 = (bf16[768,768]{1,0:T(8,128)(2,1)S(1)}, bf16[768,768]{1,0:T(8,128)(2,1)}, u32[]{:S(2)}) copy-start(bf16[768,768]{1,0:T(8,128)(2,1)} %param.10) | copy-start | bytes 3538948
  22.4 10.4 %copy-start.17 = (pred[7,32]{1,0:T(8,128)(4,1)}, pred[7,32]{1,0:T(8,128)(4,1)S(1)}, u32[]{:S(2)}) copy-start(pred[7,32]{1,0:T(8,128)(4,1)S(1)} %get-tuple-element.53) | copy-start | bytes 676
  22.4 10.4 %copy-start.18 = (pred[7,32]{1,0:T(8,128)(4,1)}, pred[7,32]{1,0:T(8,128)(4,1)S(1)}, u32[]{:S(2)}) copy-start(pred[7,32]{1,0:T(8,128)(4,1)S(1)} %get-tuple-element.54) | copy-start | bytes 676
  25.7 31.4 %collective-permute-start = (bf16[4,32,2304]{2,1,0:T(8,128)(2,1)}, bf16[4,32,2304]{2,1,0:T(8,128)(2,1)}, u32[]{:S(2)}, u32[]{:S(2)}) collective-permute-start(bf16[4,32,2304]{2,1,0:T(8,128)(2,1)} %slice.347), channel_id=1, source_target_pairs={{0,16},{1,17},{2,18},{3,19},{4,20},{5,21},{6,22},{7,23},{8,24},{9,... | collective-permute-start | bytes 1769480 | tf_op jit(solution)/shard_map/ppermute | solution.py:17
  37.6 10.0 %collective-permute-start.6 = (bf16[4,32,768]{2,1,0:T(8,128)(2,1)}, bf16[4,32,768]{2,1,0:T(8,128)(2,1)}, u32[]{:S(2)}, u32[]{:S(2)}) collective-permute-start(bf16[4,32,768]{2,1,0:T(8,128)(2,1)} %slice.378), channel_id=1, source_target_pairs={{0,16},{1,17},{2,18},{3,19},{4,20},{5,21},{6,22},{7,23},{8,24},{9,... | collective-permute-start | bytes 589832 | tf_op jit(solution)/shard_map/ppermute | solution.py:17
  43.2 26.1 %slice-start = ((bf16[7,32,2304]{2,1,0:T(8,128)(2,1)}), bf16[1,32,2304]{2,1,0:T(8,128)(2,1)S(1)}, s32[]{:S(2)}) async-start(bf16[7,32,2304]{2,1,0:T(8,128)(2,1)} %copy-done.4), calls=%async_computation.4 | async-start | bytes 294912 | tf_op jit(solution)/shard_map/slice | solution.py:36
  49.4 3.3 collective-permute-start.7
  53.6 10.9 %collective-permute-start.8 = (bf16[4,32,768]{2,1,0:T(8,128)(2,1)S(1)}, bf16[4,32,768]{2,1,0:T(8,128)(2,1)S(1)}, u32[]{:S(2)}, u32[]{:S(2)}) collective-permute-start(bf16[4,32,768]{2,1,0:T(8,128)(2,1)S(1)} %pad_maximum_fusion.12), channel_id=1, source_target_pairs={{0,1},{1,2},{2,3},{4,5},{5,6},{6,7},{8,9},{9,10},{10,11},{12,13},{... | collective-permute-start | bytes 589832 | tf_op jit(solution)/shard_map/ppermute | solution.py:17
  59.1 9.3 %collective-permute-start.1 = (bf16[4,32,2304]{2,1,0:T(8,128)(2,1)S(1)}, bf16[4,32,2304]{2,1,0:T(8,128)(2,1)S(1)}, u32[]{:S(2)}, u32[]{:S(2)}) collective-permute-start(bf16[4,32,2304]{2,1,0:T(8,128)(2,1)S(1)} %pad_maximum_fusion.2), channel_id=1, source_target_pairs={{0,4},{4,8},{8,12},{1,5},{5,9},{9,13},{2,6},{6,10},{10,14},{3,7},{... | collective-permute-start | bytes 1769480 | tf_op jit(solution)/shard_map/ppermute | solution.py:17
  70.2 17.5 %collective-permute-start.2 = (bf16[4,32,2304]{2,1,0:T(8,128)(2,1)}, bf16[4,32,2304]{2,1,0:T(8,128)(2,1)}, u32[]{:S(2)}, u32[]{:S(2)}) collective-permute-start(bf16[4,32,2304]{2,1,0:T(8,128)(2,1)} %pad_maximum_fusion.3), channel_id=1, source_target_pairs={{0,1},{1,2},{2,3},{4,5},{5,6},{6,7},{8,9},{9,10},{10,11},{12,13},{... | collective-permute-start | bytes 1769480 | tf_op jit(solution)/shard_map/ppermute | solution.py:17
  152.8 21.8 %collective-permute-start.3 = (bf16[4,32,768]{2,1,0:T(8,128)(2,1)}, bf16[4,32,768]{2,1,0:T(8,128)(2,1)}, u32[]{:S(2)}, u32[]{:S(2)}) collective-permute-start(bf16[4,32,768]{2,1,0:T(8,128)(2,1)} %pad_maximum_fusion.8), channel_id=1, source_target_pairs={{1,0},{2,1},{3,2},{5,4},{6,5},{7,6},{9,8},{10,9},{11,10},{13,12},{... | collective-permute-start | bytes 589832 | tf_op jit(solution)/shard_map/ppermute | solution.py:17
  171.0 11.7 %copy-start.13 = (bf16[1,32,768]{2,1,0:T(8,128)(2,1)S(1)}, bf16[1,32,768]{2,1,0:T(8,128)(2,1)}, u32[]{:S(2)}) copy-start(bf16[1,32,768]{2,1,0:T(8,128)(2,1)} %get-tuple-element.19) | copy-start | bytes 147460
  173.2 15.2 %collective-permute-start.9 = (bf16[4,32,2304]{2,1,0:T(8,128)(2,1)S(1)}, bf16[4,32,2304]{2,1,0:T(8,128)(2,1)S(1)}, u32[]{:S(2)}, u32[]{:S(2)}) collective-permute-start(bf16[4,32,2304]{2,1,0:T(8,128)(2,1)S(1)} %pad_maximum_fusion.4), channel_id=1, source_target_pairs={{1,0},{2,1},{3,2},{5,4},{6,5},{7,6},{9,8},{10,9},{11,10},{13,12},{... | collective-permute-start | bytes 1769480 | tf_op jit(solution)/shard_map/ppermute | solution.py:17
  175.5 7.3 %collective-permute-start.4 = (bf16[4,32,768]{2,1,0:T(8,128)(2,1)S(1)}, bf16[4,32,768]{2,1,0:T(8,128)(2,1)S(1)}, u32[]{:S(2)}, u32[]{:S(2)}) collective-permute-start(bf16[4,32,768]{2,1,0:T(8,128)(2,1)S(1)} %pad_maximum_fusion.9), channel_id=1, source_target_pairs={{4,0},{8,4},{12,8},{5,1},{9,5},{13,9},{6,2},{10,6},{14,10},{7,3},{... | collective-permute-start | bytes 589832 | tf_op jit(solution)/shard_map/ppermute | solution.py:17
  182.8 7.6 %collective-permute-start.5 = (bf16[4,32,768]{2,1,0:T(8,128)(2,1)S(1)}, bf16[4,32,768]{2,1,0:T(8,128)(2,1)S(1)}, u32[]{:S(2)}, u32[]{:S(2)}) collective-permute-start(bf16[4,32,768]{2,1,0:T(8,128)(2,1)S(1)} %pad_maximum_fusion.10), channel_id=1, source_target_pairs={{16,0},{17,1},{18,2},{19,3},{20,4},{21,5},{22,6},{23,7},{24,8},{25... | collective-permute-start | bytes 589832 | tf_op jit(solution)/shard_map/ppermute | solution.py:17
  197.1 229.9 %reduce-scatter.3.cloned.1.call-start = ((), (), s32[]{:S(2)}) async-start(), calls=%async_computation.2 | async-start | bytes 7299072 | tf_op jit(solution)/shard_map/reduce_scatter | solution.py:138
  197.1 9.2 %copy-start.9 = (bf16[1,32,2304]{2,1,0:T(8,128)(2,1)S(1)}, bf16[1,32,2304]{2,1,0:T(8,128)(2,1)}, u32[]{:S(2)}) copy-start(bf16[1,32,2304]{2,1,0:T(8,128)(2,1)} %get-tuple-element.12) | copy-start | bytes 442372
  197.1 9.2 %copy-start.11 = (bf16[1,32,2304]{2,1,0:T(8,128)(2,1)S(1)}, bf16[1,32,2304]{2,1,0:T(8,128)(2,1)}, u32[]{:S(2)}) copy-start(bf16[1,32,2304]{2,1,0:T(8,128)(2,1)} %get-tuple-element.27) | copy-start | bytes 442372
  197.1 21.0 %copy-start.10 = (bf16[1,32,2304]{2,1,0:T(8,128)(2,1)S(1)}, bf16[1,32,2304]{2,1,0:T(8,128)(2,1)}, u32[]{:S(2)}) copy-start(bf16[1,32,2304]{2,1,0:T(8,128)(2,1)} %get-tuple-element.26) | copy-start | bytes 442372
  198.4 7.8 %collective-permute-start.10 = (bf16[4,32,2304]{2,1,0:T(8,128)(2,1)S(1)}, bf16[4,32,2304]{2,1,0:T(8,128)(2,1)S(1)}, u32[]{:S(2)}, u32[]{:S(2)}) collective-permute-start(bf16[4,32,2304]{2,1,0:T(8,128)(2,1)S(1)} %pad_maximum_fusion.5), channel_id=1, source_target_pairs={{4,0},{8,4},{12,8},{5,1},{9,5},{13,9},{6,2},{10,6},{14,10},{7,3},{... | collective-permute-start | bytes 1769480 | tf_op jit(solution)/shard_map/ppermute | solution.py:17
  206.3 17.1 %copy-start.16 = (f32[768]{0:T(1024)S(1)}, f32[768]{0:T(1024)}, u32[]{:S(2)}) copy-start(f32[768]{0:T(1024)} %param.8) | copy-start | bytes 9220
  206.4 11.8 %collective-permute-start.11 = (bf16[4,32,2304]{2,1,0:T(8,128)(2,1)S(1)}, bf16[4,32,2304]{2,1,0:T(8,128)(2,1)S(1)}, u32[]{:S(2)}, u32[]{:S(2)}) collective-permute-start(bf16[4,32,2304]{2,1,0:T(8,128)(2,1)S(1)} %pad_maximum_fusion.6), channel_id=1, source_target_pairs={{16,0},{17,1},{18,2},{19,3},{20,4},{21,5},{22,6},{23,7},{24,8},{25... | collective-permute-start | bytes 1769480 | tf_op jit(solution)/shard_map/ppermute | solution.py:17
  (14 other events, 49.9 us)
Sparse Core Ops, SparseCore 0:
  197.2 104.3 reduce-scatter.4
  308.8 118.1 reduce-scatter.2
where the time goes:
time: 441 us; the launch traced here: 434 us
  waiting for transfers between devices  170 us (39%)
  local copies, waits for them, and re-layouts  99.1 us (22%)
  blocking collectives  47.2 us (11%)
  matrix products  43.8 us (10%)
  other arithmetic  29.6 us (7%)
  starting transfers between devices  29.5 us (7%)
  between operations  14.8 us (3%)
    reduce_scatter x1, waiting for transfers between devices, on_device(): lax.psum_scatter(grad_qkv, ('gx', 'gy', 'gz'), scatter_dimension=0, tiled...  125 us
    unnamed x1, blocking collectives  47.2 us
    gather x8, local copies, waits for them, and re-layouts, gather_rows(): taken = jnp.take(table, safe, axis=0)  34.1 us
    ppermute x12, waiting for transfers between devices, passed_along(): lax.ppermute(value, axis, [(source, source + steps) for source in range(i...  31.6 us
    ppermute x12, starting transfers between devices, passed_along(): lax.ppermute(value, axis, [(source, source + steps) for source in range(i...  29.4 us
    unnamed x62, local copies, waits for them, and re-layouts  20.8 us
    scatter x4, local copies, waits for them, and re-layouts, spread_rows(): return empty.at[target].set(values, mode='drop')  17.5 us
    reduce_scatter x1, waiting for transfers between devices, on_device(): lax.psum_scatter(grad_proj, ('gx', 'gy', 'gz'), scatter_dimension=0, tile...  13.1 us
  transfers between devices with their start and end apart: 14, of which 8 were waited for; matrix products, arithmetic and copies ran while one was open for 19% of the time, Pallas kernels for 0%

commit v1 on v0

v1 whole, which is shorter than its diff:
```python
import functools

import jax
import jax.numpy as jnp
from jax import lax
from jax.experimental import pallas as pl
from jax.experimental.pallas import tpu as pltpu
from jax.sharding import PartitionSpec as P

HEADS = 12
WCAP = 128
COLS = 256
VMEM_BYTES = 56 * 1024 * 1024

epsilon = 1e-06
big_negative = -1e30

AXES = ("gx", "gy", "gz")
MESH = pl.DeviceIdType.MESH
f32 = jnp.float32
bf16 = jnp.bfloat16


def nn(a, b):
    return lax.dot_general(a, b, (((1,), (0,)), ((), ())), preferred_element_type=f32)


def nt(a, b):
    return lax.dot_general(a, b, (((1,), (1,)), ((), ())), preferred_element_type=f32)


def tn(a, b):
    return lax.dot_general(a, b, (((0,), (0,)), ((), ())), preferred_element_type=f32)


def direction(k):
    return (k // 4, k // 2 % 2, k % 2)


def neighbours(sizes):
    here = [lax.axis_index(a) for a in AXES]
    found = []
    for k in range(1, 8):
        step = direction(k)
        up = tuple(here[i] + step[i] for i in range(3))
        down = tuple(here[i] - step[i] for i in range(3))
        has_up = functools.reduce(
            jnp.logical_and, [up[i] < sizes[i] for i in range(3) if step[i]]
        )
        has_down = functools.reduce(
            jnp.logical_and, [down[i] >= 0 for i in range(3) if step[i]]
        )
        found.append((up, down, has_up, has_down))
    return found


def greet(found, partners):
    barrier = pltpu.get_barrier_semaphore()
    count = jnp.int32(len(partners))
    for up, down, has_up, has_down in found:
        @pl.when(has_up)
        def _():
            pl.semaphore_signal(barrier, inc=1, device_id=up, device_id_type=MESH)

        @pl.when(has_down)
        def _():
            pl.semaphore_signal(barrier, inc=1, device_id=down, device_id_type=MESH)

        count = count + has_up.astype(jnp.int32) + has_down.astype(jnp.int32)
    for partner in partners:
        pl.semaphore_signal(barrier, inc=1, device_id=partner, device_id_type=MESH)
    pl.semaphore_wait(barrier, count)


def exchange_kernel(sizes, tok_ref, gout_ref, send_ref, table_ref, buf, send_sem, recv_sem):
    found = neighbours(sizes)
    count, width = tok_ref.shape
    cap = send_ref.shape[0] // 7
    greet(found, [])
    pick = (
        lax.broadcasted_iota(jnp.int32, (7 * cap, count), 1) == send_ref[...]
    ).astype(f32).astype(bf16)
    buf[:, :width] = nn(pick, tok_ref[...]).astype(bf16)
    buf[:, width:] = nn(pick, gout_ref[...]).astype(bf16)

    def copy(k):
        return pltpu.make_async_remote_copy(
            src_ref=buf.at[pl.ds(k * cap, cap)],
            dst_ref=table_ref.at[pl.ds(count + k * cap, cap)],
            send_sem=send_sem.at[k],
            recv_sem=recv_sem.at[k],
            device_id=found[k][0],
            device_id_type=MESH,
        )

    for k in (6, 5, 4, 3, 2, 1, 0):
        @pl.when(found[k][2])
        def _():
            copy(k).start()
    table_ref[:count, :width] = tok_ref[...]
    table_ref[:count, width:] = gout_ref[...]
    for k in range(7):
        @pl.when(jnp.logical_not(found[k][3]))
        def _():
            table_ref[pl.ds(count + k * cap, cap), :] = jnp.zeros((cap, 2 * width), bf16)
    for k in range(7):
        @pl.when(found[k][3])
        def _():
            copy(k).wait_recv()

        @pl.when(found[k][2])
        def _():
            copy(k).wait_send()


def compute_kernel(
    places, table_ref, wcol_ref, wrow_ref, gain_ref, wqkv_ref, wout_ref,
    ret_ref, grad_ref, gsum_ref,
    pick, xs, unit, normed, normed_t, inv, packed, delta, mixed, mixed_t, dpacked, dnormed,
    bg, piece,
):
    span, double = table_ref.shape
    width = double // 2
    slots = wcol_ref.shape[0]
    windows = slots // WCAP
    head_dim = width // HEADS
    scale = head_dim ** (-0.5)

    pick[...] = (
        lax.broadcasted_iota(jnp.int32, (slots, span), 1) == wcol_ref[...]
    ).astype(f32).astype(bf16)

    @pl.loop(0, double // COLS)
    def _(j):
        cols = pl.ds(pl.multiple_of(j * COLS, COLS), COLS)
        xs[:, cols] = nn(pick[...], table_ref[:, cols]).astype(bf16)

    @pl.loop(0, windows)
    def _(w):
        rows = pl.ds(pl.multiple_of(w * WCAP, WCAP), WCAP)
        floats = xs[rows, :width].astype(f32)
        centred = floats - jnp.mean(floats, axis=-1, keepdims=True)
        inv_std = lax.rsqrt(jnp.mean(centred * centred, axis=-1, keepdims=True) + epsilon)
        u = centred * inv_std
        unit[rows, :] = u
        inv[rows, :] = inv_std
        normed[rows, :] = (u * gain_ref[...]).astype(bf16)

    normed_t[...] = normed[...].T

    @pl.loop(0, 3 * width // COLS)
    def _(j):
        cols = pl.ds(pl.multiple_of(j * COLS, COLS), COLS)
        packed[:, cols] = nn(normed[...], wqkv_ref[:, cols]).astype(bf16)

    @pl.loop(0, width // COLS)
    def _(j):
        cols = pl.ds(pl.multiple_of(j * COLS, COLS), COLS)
        delta[:, cols] = nt(xs[:, width:], wout_ref[cols, :]).astype(bf16)

    pair = 2 * head_dim

    @pl.loop(0, windows)
    def _(w):
        rows = pl.ds(pl.multiple_of(w * WCAP, WCAP), WCAP)
        valid = (wcol_ref[rows, :] >= 0)[None]
        first = lax.broadcasted_iota(jnp.int32, (WCAP, pair), 1) < head_dim
        none = jnp.zeros((WCAP, pair), bf16)

        def split(t):
            return jnp.concatenate([jnp.where(first, t, none), jnp.where(first, none, t)], axis=0)

        def join(t):
            return jnp.where(first, t[:WCAP], t[WCAP:])

        for j in range(HEADS // 2):
            at = j * pair
            q = packed[rows, at:at + pair]
            k2 = split(packed[rows, width + at:width + at + pair])
            v2 = split(packed[rows, 2 * width + at:2 * width + at + pair])
            g = delta[rows, at:at + pair]
            scores = nt(k2, q).reshape(2, WCAP, WCAP) * scale
            scores = jnp.where(valid, scores, big_negative)
            top = jnp.max(scores, axis=1, keepdims=True)
            expo = jnp.exp(scores - top)
            probs = expo * (1.0 / jnp.sum(expo, axis=1, keepdims=True))
            weights = probs.reshape(2 * WCAP, WCAP).astype(bf16)
            mixed[rows, at:at + pair] = tn(weights, v2).astype(bf16)
            dweights = nt(v2, g).reshape(2, WCAP, WCAP)
            total = jnp.sum(dweights * probs, axis=1, keepdims=True)
            dscaled = (probs * (dweights - total) * scale).reshape(2 * WCAP, WCAP).astype(bf16)
            dpacked[rows, at:at + pair] = tn(dscaled, k2).astype(bf16)
            dpacked[rows, width + at:width + at + pair] = join(nn(dscaled, q)).astype(bf16)
            dpacked[rows, 2 * width + at:2 * width + at + pair] = join(nn(weights, g)).astype(bf16)

    mixed_t[...] = mixed[...].T

    @pl.loop(0, width // COLS)
    def _(j):
        cols = pl.ds(pl.multiple_of(j * COLS, COLS), COLS)
        out = nn(mixed[...], wout_ref[:, cols])
        bg[:, cols] = (xs[:, cols].astype(f32) + out).astype(bf16)
        dnormed[:, cols] = nt(dpacked[...], wqkv_ref[cols, :]).astype(bf16)

    gsum_ref[...] = jnp.zeros_like(gsum_ref)

    @pl.loop(0, windows)
    def _(w):
        rows = pl.ds(pl.multiple_of(w * WCAP, WCAP), WCAP)
        dn = dnormed[rows, :].astype(f32)
        u = unit[rows, :]
        gsum_ref[...] += jnp.sum((dn * u).reshape(WCAP // 8, 8, width), axis=0)
        dunit = dn * gain_ref[...]
        dcentre = inv[rows, :] * (
            dunit
            - jnp.mean(dunit, axis=-1, keepdims=True)
            - u * jnp.mean(dunit * u, axis=-1, keepdims=True)
        )
        bg[rows, width:] = (xs[rows, width:].astype(f32) + dcentre).astype(bf16)

    back = (
        lax.broadcasted_iota(jnp.int32, (span, slots), 0) == wrow_ref[...]
    ).astype(f32).astype(bf16)
    pick_t = back

    for j in range(double // COLS):
        ret_ref[:, j * COLS:(j + 1) * COLS] = nn(pick_t, bg[:, j * COLS:(j + 1) * COLS]).astype(bf16)

    def gradient(j):
        if j < 3 * width // COLS:
            return nn(normed_t[...], dpacked[:, j * COLS:(j + 1) * COLS])
        at = j * COLS - 3 * width
        return nn(mixed_t[...], xs[:, width + at:width + at + COLS])

    if places is None:
        for j in range(4 * width // COLS):
            grad_ref[:, j * COLS:(j + 1) * COLS] = gradient(j)
        return
    rows = grad_ref.shape[2] // 2
    for p, place in enumerate(places):
        piece[0] = gradient(2 * p)
        piece[1] = gradient(2 * p + 1)
        for c, position in enumerate(place):
            both = jnp.concatenate(
                [piece[0, c * rows:(c + 1) * rows, :], piece[1, c * rows:(c + 1) * rows, :]], axis=0
            )
            grad_ref[p, position] = both.astype(bf16)


def finish_kernel(sizes, orders, bits, *refs):
    parts = len(orders)
    stages = len(bits)
    refs = list(refs)
    ret_ref, srow_ref, gsum_ref = refs[:3]
    refs = refs[3:]
    if parts:
        grad_ref = refs.pop(0)
    block_ref, gtok_ref, gain_ref = refs[:3]
    refs = refs[3:]
    if parts:
        gqkv_ref, gout_ref = refs[:2]
        refs = refs[2:]
    back, gheld, gcome, ret_send, ret_recv, gain_send, gain_recv = refs[:7]
    refs = refs[7:]
    if parts:
        part_send, part_recv = refs[:2]
        come = refs[2:2 + stages]
        held = [grad_ref] + list(refs[2 + stages:])

    found = neighbours(sizes)
    count, width = block_ref.shape
    cap = back.shape[0] // 7
    here = [lax.axis_index(a) for a in AXES]

    def own_bit(bit):
        axis, distance = bit
        return here[axis] // distance % 2

    def partner(bit):
        axis, distance = bit
        return tuple(
            here[i] + distance * (1 - 2 * own_bit(bit)) if i == axis else here[i] for i in range(3)
        )

    greet(found, [partner(bit) for bit in bits])

    def return_copy(k):
        return pltpu.make_async_remote_copy(
            src_ref=ret_ref.at[pl.ds(count + k * cap, cap)],
            dst_ref=back.at[pl.ds(k * cap, cap)],
            send_sem=ret_send.at[k],
            recv_sem=ret_recv.at[k],
            device_id=found[k][1],
            device_id_type=MESH,
        )

    def part_copy(p, s):
        bit = orders[p][s]
        half = come[s].shape[1]
        return pltpu.make_async_remote_copy(
            src_ref=held[s].at[p, pl.ds((1 - own_bit(bit)) * half, half)],
            dst_ref=come[s].at[p],
            send_sem=part_send.at[p * stages + s],
            recv_sem=part_recv.at[p * stages + s],
            device_id=partner(bit),
            device_id_type=MESH,
        )

    def gain_copy(s):
        return pltpu.make_async_remote_copy(
            src_ref=gsum_ref if s == 0 else gheld.at[s - 1],
            dst_ref=gcome.at[s],
            send_sem=gain_send.at[s],
            recv_sem=gain_recv.at[s],
            device_id=partner(bits[s]),
            device_id_type=MESH,
        )

    for p in range(parts):
        part_copy(p, 0).start()
    gain_copy(0).start()
    for k in (6, 5, 4, 3, 2, 1, 0):
        @pl.when(found[k][3])
        def _():
            return_copy(k).start()
    for k in range(7):
        @pl.when(jnp.logical_not(found[k][2]))
        def _():
            back[pl.ds(k * cap, cap), :] = jnp.zeros((cap, 2 * width), bf16)

    for s in range(stages):
        for p in range(parts):
            part_copy(p, s).wait_recv()
            half = come[s].shape[1]
            base = own_bit(orders[p][s]) * half
            if s < stages - 1:
                step = min(half, 2)

                @pl.loop(0, half // step)
                def _(i):
                    mine = held[s][p, pl.ds(base + i * step, step)].astype(f32)
                    theirs = come[s][p, pl.ds(i * step, step)].astype(f32)
                    held[s + 1][p, pl.ds(i * step, step)] = (mine + theirs).astype(bf16)

                part_copy(p, s + 1).start()
            else:
                mine = held[s][p, pl.ds(base, 1)].astype(f32)
                total = mine[0] + come[s][p, 0].astype(f32)
                rows = total.shape[0] // 2
                for i in range(2):
                    at = (2 * p + i) * COLS
                    value = total[i * rows:(i + 1) * rows]
                    if at < 3 * width:
                        gqkv_ref[:, at:at + COLS] = value
                    else:
                        gout_ref[:, at - 3 * width:at - 3 * width + COLS] = value
        gain_copy(s).wait_recv()
        total = (gsum_ref[...] if s == 0 else gheld[s - 1]) + gcome[s]
        if s < stages - 1:
            gheld[s] = total
            gain_copy(s + 1).start()
        else:
            gain_ref[...] = total

    for k in range(7):
        @pl.when(found[k][2])
        def _():
            return_copy(k).wait_recv()
    place = (
        lax.broadcasted_iota(jnp.int32, (count, 7 * cap), 0) == srow_ref[...]
    ).astype(f32).astype(bf16)
    block_ref[...] = (
        ret_ref[:count, :width].astype(f32) + nn(place, back[:, :width])
    ).astype(bf16)
    gtok_ref[...] = (
        ret_ref[:count, width:].astype(f32) + nn(place, back[:, width:])
    ).astype(bf16)

    for k in range(7):
        @pl.when(found[k][3])
        def _():
            return_copy(k).wait_send()
    for s in range(stages):
        for p in range(parts):
            part_copy(p, s).wait_send()
        gain_copy(s).wait_send()


def on_device(sizes, tokens, norm_gain, w_qkv, w_out, send_rows, window_rows, grad_out):
    count, width = tokens.shape
    slots = window_rows.shape[1]
    cap = send_rows.shape[2]
    span = count + 7 * cap
    devices = sizes[0] * sizes[1] * sizes[2]
    vmem = pl.BlockSpec(memory_space=pltpu.VMEM)
    params = functools.partial(pltpu.CompilerParams, vmem_limit_bytes=VMEM_BYTES)

    by_axis = [[(a, 1 << i) for i in range(sizes[a].bit_length() - 1)] for a in range(3)]
    x_bits, y_bits, z_bits = by_axis
    bits = y_bits + x_bits + z_bits
    chunk = width // devices
    grouped = (
        all(1 << len(b) == n for b, n in zip(by_axis, sizes))
        and len(y_bits) > 0
        and chunk * devices == width
        and chunk % 8 == 0
    )
    parts = 4 * width // (2 * COLS)
    orders, places = [], None
    if grouped:
        rest = y_bits[1:]
        kinds = [
            y_bits[:1] + x_bits + rest + z_bits,
            y_bits[:1] + rest + z_bits + x_bits,
            y_bits[:1] + z_bits + x_bits + rest,
        ]
        orders = [kinds[p % 3] for p in range(parts)]

        def position(order, c):
            at = (c // (sizes[1] * sizes[2]), c // sizes[2] % sizes[1], c % sizes[2])
            value = 0
            for axis, distance in order:
                value = 2 * value + at[axis] // distance % 2
            return value

        places = [[position(order, c) for c in range(devices)] for order in orders]

    send_flat = send_rows.reshape(7 * cap)
    send_col = send_flat.reshape(7 * cap, 1)
    send_row = send_flat.reshape(1, 7 * cap)
    slot_col = window_rows.reshape(slots, 1)

    table = pl.pallas_call(
        functools.partial(exchange_kernel, sizes),
        out_shape=jax.ShapeDtypeStruct((span, 2 * width), bf16),
        in_specs=[vmem] * 3,
        out_specs=vmem,
        scratch_shapes=[
            pltpu.VMEM((7 * cap, 2 * width), bf16),
            pltpu.SemaphoreType.DMA((7,)),
            pltpu.SemaphoreType.DMA((7,)),
        ],
        compiler_params=params(collective_id=0, has_side_effects=True),
        name="exchange",
    )(tokens, grad_out, send_col)

    if grouped:
        grad_shape = jax.ShapeDtypeStruct((parts, devices, 2 * chunk, COLS), bf16)
    else:
        grad_shape = jax.ShapeDtypeStruct((width, 4 * width), f32)
    ret, grads, gsum = pl.pallas_call(
        functools.partial(compute_kernel, places),
        out_shape=(
            jax.ShapeDtypeStruct((span, 2 * width), bf16),
            grad_shape,
            jax.ShapeDtypeStruct((8, width), f32),
        ),
        in_specs=[vmem] * 6,
        out_specs=(vmem,) * 3,
        scratch_shapes=[
            pltpu.VMEM((slots, span), bf16),
            pltpu.VMEM((slots, 2 * width), bf16),
            pltpu.VMEM((slots, width), f32),
            pltpu.VMEM((slots, width), bf16),
            pltpu.VMEM((width, slots), bf16),
            pltpu.VMEM((slots, 1), f32),
            pltpu.VMEM((slots, 3 * width), bf16),
            pltpu.VMEM((slots, width), bf16),
            pltpu.VMEM((slots, width), bf16),
            pltpu.VMEM((width, slots), bf16),
            pltpu.VMEM((slots, 3 * width), bf16),
            pltpu.VMEM((slots, width), bf16),
            pltpu.VMEM((slots, 2 * width), bf16),
            pltpu.VMEM((2, width, COLS), f32),
        ],
        compiler_params=params(),
        name="windows",
    )(table, slot_col, window_rows, norm_gain.reshape(1, width), w_qkv, w_out)

    stages = len(bits)
    out_shape = [
        jax.ShapeDtypeStruct((count, width), bf16),
        jax.ShapeDtypeStruct((count, width), bf16),
        jax.ShapeDtypeStruct((8, width), f32),
    ]
    scratch = [
        pltpu.VMEM((7 * cap, 2 * width), bf16),
        pltpu.VMEM((stages, 8, width), f32),
        pltpu.VMEM((stages, 8, width), f32),
        pltpu.SemaphoreType.DMA((7,)),
        pltpu.SemaphoreType.DMA((7,)),
        pltpu.SemaphoreType.DMA((stages,)),
        pltpu.SemaphoreType.DMA((stages,)),
    ]
    operands = [ret, send_row, gsum]
    if grouped:
        out_shape += [
            jax.ShapeDtypeStruct((chunk, 3 * width), f32),
            jax.ShapeDtypeStruct((chunk, width), f32),
        ]
        scratch += [pltpu.SemaphoreType.DMA((parts * stages,))] * 2
        slab = (2 * chunk, COLS)
        scratch += [pltpu.VMEM((parts, devices >> (s + 1)) + slab, bf16) for s in range(stages)]
        scratch += [pltpu.VMEM((parts, devices >> s) + slab, bf16) for s in range(1, stages)]
        operands.append(grads)
    outs = pl.pallas_call(
        functools.partial(finish_kernel, sizes, orders, bits),
        out_shape=tuple(out_shape),
        in_specs=[vmem] * len(operands),
        out_specs=(vmem,) * len(out_shape),
        scratch_shapes=scratch,
        compiler_params=params(collective_id=1, has_side_effects=True),
        name="finish",
    )(*operands)
    block_out, grad_tokens, gain_sum = outs[:3]
    me = (lax.axis_index("gx") * sizes[1] + lax.axis_index("gy")) * sizes[2] + lax.axis_index("gz")
    grad_gain = jnp.sum(lax.dynamic_slice_in_dim(gain_sum, me * chunk, chunk, axis=1), axis=0)
    if grouped:
        grad_qkv, grad_proj = outs[3:]
    else:
        summed = lax.psum_scatter(grads, AXES, scatter_dimension=0, tiled=True)
        grad_qkv, grad_proj = summed[:, :3 * width], summed[:, 3 * width:]
    return (block_out, grad_tokens, grad_gain, grad_qkv, grad_proj)


def solution(mesh):
    sizes = tuple(mesh.shape[a] for a in AXES)
    in_specs = (
        P(AXES, None),
        P(),
        P(),
        P(),
        P(AXES, None, None),
        P(AXES, None),
        P(AXES, None),
    )
    out_specs = (
        P(AXES, None),
        P(AXES, None),
        P(AXES),
        P(AXES, None),
        P(AXES, None),
    )
    return jax.shard_map(
        functools.partial(on_device, sizes),
        mesh=mesh,
        in_specs=in_specs,
        out_specs=out_specs,
        check_vma=False,
    )
```

time: 441 us -> 101 us (0.23); the launches traced: 434 us -> 100 us
  waiting for transfers between devices: 170 us -> 0 us
  local copies, waits for them, and re-layouts: 99.1 us -> 9.07 us
  Pallas kernels: 0 us -> 88.5 us
  blocking collectives: 47.2 us -> 0 us
  matrix products: 43.8 us -> 0 us
  starting transfers between devices: 29.5 us -> 0 us
  other arithmetic: 29.6 us -> 2.04 us
  between operations: 14.8 us -> 0.68 us
    reduce_scatter x2 -> x0, waiting for transfers between devices: 139 us -> none  [the longest x1 125 us: on_device(): lax.psum_scatter(grad_qkv, ('gx', 'gy', 'gz'), scatter_dimension=0, tiled...]
    pallas_call x0 -> x3, Pallas kernels: none -> 88.5 us  [the longest x1 44.1 us: on_device(): pl.pallas_call(functools.partial(finish_kernel, sizes, orders, bits), out...]
    unnamed x1 -> x0, blocking collectives: 47.2 us -> none
    dot_general x12 -> x0, matrix products: 43.8 us -> none  [the longest x1 6.92 us: attend_back(): jnp.einsum('whqk,wqhd->wkhd', dscaled, query, preferred_element_type=jnp....]
    gather x8 -> x0, local copies, waits for them, and re-layouts: 34.1 us -> none  [gather_rows(): taken = jnp.take(table, safe, axis=0)]
    ppermute x12 -> x0, waiting for transfers between devices: 31.6 us -> none  [passed_along(): lax.ppermute(value, axis, [(source, source + steps) for source in range(i...]
    ppermute x12 -> x0, starting transfers between devices: 29.4 us -> none  [passed_along(): lax.ppermute(value, axis, [(source, source + steps) for source in range(i...]
    scatter x4 -> x0, local copies, waits for them, and re-layouts: 17.5 us -> none  [spread_rows(): return empty.at[target].set(values, mode='drop')]
  transfers between devices with their start and end apart: 14 -> 0, of which waited for: 8 -> 0; matrix products, arithmetic and copies ran while one was open for 19% -> 0% of each run, Pallas kernels for 0% -> 0%
where the time goes in v1:
time: 101 us; the launch traced here: 100 us
  Pallas kernels  88.5 us (88%)
  local copies, waits for them, and re-layouts  9.07 us (9%)
  other arithmetic  2.04 us (2%)
    pallas_call x1, Pallas kernels, on_device(): pl.pallas_call(functools.partial(finish_kernel, sizes, orders, bits), out...  44.1 us
    pallas_call x1, Pallas kernels, on_device(): pl.pallas_call(functools.partial(compute_kernel, places), out_shape=(jax....  28.4 us
    pallas_call x1, Pallas kernels, on_device(): pl.pallas_call(functools.partial(exchange_kernel, sizes), out_shape=jax.S...  16 us
    unnamed x8, local copies, waits for them, and re-layouts  4.86 us

profile of v1, /device:TPU:0, one launch (start us, length us, event | category | flops | bytes accessed | tf_op | source)
XLA Modules:
  0.0 100.2 jit_solution(18443755190515865970)
XLA Ops:
  0.6 1.3 %reshape.17.gain_ref = f32[1,768]{1,0:T(1,128)} reshape(f32[768]{0:T(1024)} %param.8) | data formatting | bytes 6144 | tf_op jit(solution)/shard_map/reshape | solution.py:478
  1.9 0.7 reduce
  2.6 0.6 reshape_reshape.7.refs_1_
  3.3 0.8 reshape_reshape.8.send_ref
  4.0 1.5 %copy.13.wcol_ref = s32[512,1]{1,0:T(8,128)} copy(s32[512,1]{0,1:T(1,128)} %bitcast.1) | data formatting | bytes 4096 | tf_op jit(solution)/shard_map/reshape | solution.py:431
  5.6 16.0 %exchange.1.table_ref = bf16[480,1536]{1,0:T(8,128)(2,1)} custom-call(bf16[256,768]{1,0:T(8,128)(2,1)} %tok_ref.1, bf16[256,768]{1,0:T(8,128)(2,1)} %gout_ref.1, s32[224,1]{1,0:T(8,128)} %reshape_reshape.8.send_ref), custom_call_target="tpu_custom_call" | custom-call | tf_op jit(solution)/shard_map/exchange/pallas_call | solution.py:433
  21.6 28.4 %windows.1 = (bf16[480,1536]{1,0:T(8,128)(2,1)}, bf16[6,32,48,256]{3,2,1,0:T(8,128)(2,1)}, f32[8,768]{1,0:T(8,128)}) custom-call(bf16[480,1536]{1,0:T(8,128)(2,1)} %exchange.1.table_ref, s32[512,1]{1,0:T(8,128)} %copy.13.wcol_ref, s32[1,512]{1,0:T(1,128)} %wrow_ref.1, f32[1,768]{1,0:T(1,128)} %reshape.17.gain_ref, bf16[768,2304]{1,0:T(8,128)(2,1)} %wqkv_ref.1, ...), custom_call_target="tpu_custom_call" | custom-call | tf_op jit(solution)/shard_map/windows/pallas_call | solution.py:451
  49.9 44.1 %finish.1 = (bf16[256,768]{1,0:T(8,128)(2,1)}, bf16[256,768]{1,0:T(8,128)(2,1)}, f32[8,768]{1,0:T(8,128)}, f32[24,2304]{1,0:T(8,128)}, f32[24,768]{1,0:T(8,128)}) custom-call(bf16[480,1536]{1,0:T(8,128)(2,1)} %get-tuple-element.13.refs_0_, s32[1,224]{1,0:T(1,128)} %reshape_reshape.7.refs_1_, f32[8,768]{1,0:T(8,128)} %get-tuple-element.14.refs_2_, ...), custom_call_target="tpu_custom_call" | custom-call | tf_op jit(solution)/shard_map/finish/pallas_call | solution.py:506
  94.0 0.0 copy-start
  94.0 0.0 copy-start.1
  94.0 1.3 %dynamic-slice_reduce_fusion = f32[24]{0:T(128)} fusion(f32[8,768]{1,0:T(8,128)} %get-tuple-element.18, s32[]{:T(128)S(6)} %select_n.3), kind=kLoop, calls=%fused_computation | loop fusion | flops 168 | bytes 868 | tf_op jit(solution)/shard_map/reduce_sum | solution.py:517
  95.4 1.8 %copy.18 = bf16[256,768]{1,0:T(8,128)(2,1)} copy(bf16[256,768]{1,0:T(8,128)(2,1)} %get-tuple-element.26) | data formatting | bytes 786432
  97.2 1.8 %copy.19 = bf16[256,768]{1,0:T(8,128)(2,1)} copy(bf16[256,768]{1,0:T(8,128)(2,1)} %get-tuple-element.27) | data formatting | bytes 786432
  98.9 0.0 copy-done
  98.9 0.7 copy.20
  99.6 0.0 copy-done.1
  99.6 0.6 copy.21
Async XLA Ops:
  94.0 4.9 %copy-start = (f32[24,2304]{1,0:T(8,128)S(1)}, f32[24,2304]{1,0:T(8,128)}, u32[]{:S(2)}) copy-start(f32[24,2304]{1,0:T(8,128)} %get-tuple-element.29) | copy-start | bytes 663556
  94.0 5.6 %copy-start.1 = (f32[24,768]{1,0:T(8,128)S(1)}, f32[24,768]{1,0:T(8,128)}, u32[]{:S(2)}) copy-start(f32[24,768]{1,0:T(8,128)} %get-tuple-element.30) | copy-start | bytes 221188

commit v2 on v1

v2 whole, which is shorter than its diff:
```python
import functools

import jax
import jax.numpy as jnp
from jax import lax
from jax.experimental import pallas as pl
from jax.experimental.pallas import tpu as pltpu
from jax.sharding import PartitionSpec as P

HEADS = 12
WCAP = 128
COLS = 256
HALF = 128
VMEM_BYTES = 56 * 1024 * 1024

epsilon = 1e-06
big_negative = -1e30

AXES = ("gx", "gy", "gz")
MESH = pl.DeviceIdType.MESH
f32 = jnp.float32
bf16 = jnp.bfloat16


def nn(a, b):
    return lax.dot_general(a, b, (((1,), (0,)), ((), ())), preferred_element_type=f32)


def nt(a, b):
    return lax.dot_general(a, b, (((1,), (1,)), ((), ())), preferred_element_type=f32)


def tn(a, b):
    return lax.dot_general(a, b, (((0,), (0,)), ((), ())), preferred_element_type=f32)


def direction(k):
    return (k // 4, k // 2 % 2, k % 2)


def neighbours(sizes):
    here = [lax.axis_index(a) for a in AXES]
    found = []
    for k in range(1, 8):
        step = direction(k)
        up = tuple(here[i] + step[i] for i in range(3))
        down = tuple(here[i] - step[i] for i in range(3))
        has_up = functools.reduce(
            jnp.logical_and, [up[i] < sizes[i] for i in range(3) if step[i]]
        )
        has_down = functools.reduce(
            jnp.logical_and, [down[i] >= 0 for i in range(3) if step[i]]
        )
        found.append((up, down, has_up, has_down))
    return found


def greet(found, partners):
    barrier = pltpu.get_barrier_semaphore()
    count = jnp.int32(len(partners))
    for up, down, has_up, has_down in found:
        @pl.when(has_up)
        def _():
            pl.semaphore_signal(barrier, inc=1, device_id=up, device_id_type=MESH)

        @pl.when(has_down)
        def _():
            pl.semaphore_signal(barrier, inc=1, device_id=down, device_id_type=MESH)

        count = count + has_up.astype(jnp.int32) + has_down.astype(jnp.int32)
    for partner in partners:
        pl.semaphore_signal(barrier, inc=1, device_id=partner, device_id_type=MESH)
    pl.semaphore_wait(barrier, count)


def block_kernel(sizes, orders, bits, places, *refs):
    parts, stages = len(orders), len(bits)
    refs = list(refs)

    def take(n):
        out = refs[:n]
        del refs[:n]
        return out

    tok_ref, gout_ref, send_ref, wrow_ref, gain_ref, wqkv_hbm, wout_hbm = take(7)
    own_ref, back_ref, place_ref, gsum_ref = take(4)
    if parts:
        gqkv_ref, gproj_ref = take(2)
    else:
        (grad_ref,) = take(1)
    buf, table, wqkv_ref, wout_ref, wcol, pick = take(6)
    xs, unit, normed, normed_t, inv, packed, delta, mixed, mixed_t, dpacked, dnormed = take(11)
    bg, ret = take(2)
    gheld, gcome = take(2)
    load_sem, send_sem, recv_sem, ret_send, ret_recv, gain_send, gain_recv = take(7)
    if parts:
        piece, part_send, part_recv = take(3)
        come = take(stages)
        held = take(stages)

    found = neighbours(sizes)
    count, width = tok_ref.shape
    double = 2 * width
    cap = send_ref.shape[2]
    span = count + 7 * cap
    slots = wrow_ref.shape[1]
    windows = slots // WCAP
    head_dim = width // HEADS
    pair = 2 * head_dim
    scale = head_dim ** (-0.5)
    here = [lax.axis_index(a) for a in AXES]

    def own_bit(bit):
        axis, distance = bit
        return here[axis] // distance % 2

    def partner(bit):
        axis, distance = bit
        return tuple(
            here[i] + distance * (1 - 2 * own_bit(bit)) if i == axis else here[i] for i in range(3)
        )

    def forward_copy(k):
        return pltpu.make_async_remote_copy(
            src_ref=buf.at[pl.ds(k * cap, cap)],
            dst_ref=table.at[pl.ds(count + k * cap, cap)],
            send_sem=send_sem.at[k],
            recv_sem=recv_sem.at[k],
            device_id=found[k][0],
            device_id_type=MESH,
        )

    def return_copy(k):
        return pltpu.make_async_remote_copy(
            src_ref=ret.at[pl.ds(k * cap, cap)],
            dst_ref=back_ref.at[pl.ds(k * cap, cap)],
            send_sem=ret_send.at[k],
            recv_sem=ret_recv.at[k],
            device_id=found[k][1],
            device_id_type=MESH,
        )

    def part_copy(p, s):
        bit = orders[p][s]
        half = come[s].shape[1]
        return pltpu.make_async_remote_copy(
            src_ref=held[s].at[p, pl.ds((1 - own_bit(bit)) * half, half)],
            dst_ref=come[s].at[p],
            send_sem=part_send.at[p * stages + s],
            recv_sem=part_recv.at[p * stages + s],
            device_id=partner(bit),
            device_id_type=MESH,
        )

    def gain_copy(s):
        return pltpu.make_async_remote_copy(
            src_ref=gheld.at[s],
            dst_ref=gcome.at[s],
            send_sem=gain_send.at[s],
            recv_sem=gain_recv.at[s],
            device_id=partner(bits[s]),
            device_id_type=MESH,
        )

    loads = [
        pltpu.make_async_copy(wqkv_hbm, wqkv_ref, load_sem.at[0]),
        pltpu.make_async_copy(wout_hbm, wout_ref, load_sem.at[1]),
    ]
    for load in loads:
        load.start()

    send_row = jnp.concatenate([send_ref[0, k:k + 1, :] for k in range(7)], axis=1)
    place = (
        lax.broadcasted_iota(jnp.int32, (count, 7 * cap), 0) == send_row
    ).astype(f32).astype(bf16)
    place_ref[...] = place
    buf[:, :width] = tn(place, tok_ref[...]).astype(bf16)
    buf[:, width:] = tn(place, gout_ref[...]).astype(bf16)
    greet(found, [partner(bit) for bit in bits])
    for k in (6, 5, 4, 3, 2, 1, 0):
        @pl.when(found[k][2])
        def _():
            forward_copy(k).start()
    table[:count, :width] = tok_ref[...]
    table[:count, width:] = gout_ref[...]
    for k in range(7):
        @pl.when(jnp.logical_not(found[k][3]))
        def _():
            table[pl.ds(count + k * cap, cap), :] = jnp.zeros((cap, double), bf16)

        @pl.when(jnp.logical_not(found[k][2]))
        def _():
            back_ref[pl.ds(k * cap, cap), :] = jnp.zeros((cap, double), bf16)
    wcol[...] = jnp.broadcast_to(wrow_ref[...], (8, slots)).T[:, :1]
    pick[...] = (
        lax.broadcasted_iota(jnp.int32, (slots, span), 1) == wcol[...]
    ).astype(f32).astype(bf16)
    gain_row = gain_ref[...].reshape(1, width)
    for load in loads:
        load.wait()
    for k in range(7):
        @pl.when(found[k][3])
        def _():
            forward_copy(k).wait_recv()

        @pl.when(found[k][2])
        def _():
            forward_copy(k).wait_send()

    @pl.loop(0, double // COLS)
    def _(j):
        cols = pl.ds(pl.multiple_of(j * COLS, COLS), COLS)
        xs[:, cols] = nn(pick[...], table[:, cols]).astype(bf16)

    @pl.loop(0, windows)
    def _(w):
        rows = pl.ds(pl.multiple_of(w * WCAP, WCAP), WCAP)
        floats = xs[rows, :width].astype(f32)
        centred = floats - jnp.mean(floats, axis=-1, keepdims=True)
        inv_std = lax.rsqrt(jnp.mean(centred * centred, axis=-1, keepdims=True) + epsilon)
        u = centred * inv_std
        unit[rows, :] = u
        inv[rows, :] = inv_std
        normed[rows, :] = (u * gain_row).astype(bf16)

    normed_t[...] = normed[...].T

    @pl.loop(0, 3 * width // COLS)
    def _(j):
        cols = pl.ds(pl.multiple_of(j * COLS, COLS), COLS)
        packed[:, cols] = nn(normed[...], wqkv_ref[:, cols]).astype(bf16)

    @pl.loop(0, width // COLS)
    def _(j):
        cols = pl.ds(pl.multiple_of(j * COLS, COLS), COLS)
        delta[:, cols] = nt(xs[:, width:], wout_ref[cols, :]).astype(bf16)

    def attention(group):
        @pl.loop(0, windows)
        def _(w):
            rows = pl.ds(pl.multiple_of(w * WCAP, WCAP), WCAP)
            valid = (wcol[rows, :] >= 0)[None]
            first = lax.broadcasted_iota(jnp.int32, (WCAP, pair), 1) < head_dim
            none = jnp.zeros((WCAP, pair), bf16)

            def split(t):
                return jnp.concatenate(
                    [jnp.where(first, t, none), jnp.where(first, none, t)], axis=0
                )

            def join(t):
                return jnp.where(first, t[:WCAP], t[WCAP:])

            for j in (2 * group, 2 * group + 1):
                at = j * pair
                q = packed[rows, at:at + pair]
                k2 = split(packed[rows, width + at:width + at + pair])
                v2 = split(packed[rows, 2 * width + at:2 * width + at + pair])
                g = delta[rows, at:at + pair]
                scores = nt(k2, q).reshape(2, WCAP, WCAP) * scale
                scores = jnp.where(valid, scores, big_negative)
                top = jnp.max(scores, axis=1, keepdims=True)
                expo = jnp.exp(scores - top)
                probs = expo * (1.0 / jnp.sum(expo, axis=1, keepdims=True))
                weights = probs.reshape(2 * WCAP, WCAP).astype(bf16)
                mixed[rows, at:at + pair] = tn(weights, v2).astype(bf16)
                dweights = nt(v2, g).reshape(2, WCAP, WCAP)
                total = jnp.sum(dweights * probs, axis=1, keepdims=True)
                dscaled = (probs * (dweights - total) * scale).reshape(2 * WCAP, WCAP).astype(bf16)
                dpacked[rows, at:at + pair] = tn(dscaled, k2).astype(bf16)
                dpacked[rows, width + at:width + at + pair] = join(nn(dscaled, q)).astype(bf16)
                dpacked[rows, 2 * width + at:2 * width + at + pair] = join(
                    nn(weights, g)
                ).astype(bf16)

    def first_column(p):
        return (p % 3) * width + (p // 3) * COLS if p < parts - 3 else 3 * width + (p - parts + 3) * COLS

    def gradient(at):
        if at < 3 * width:
            return nn(normed_t[...], dpacked[:, at:at + COLS])
        return nn(mixed_t[...], xs[:, at - 2 * width:at - 2 * width + COLS])

    def open_parts(members):
        for p in members:
            piece[p % 2] = gradient(first_column(p))
            rows = held[0].shape[2] // 2
            for c, position in enumerate(places[p]):
                both = piece[p % 2, c * rows:(c + 1) * rows, :]
                held[0][p, position] = jnp.concatenate(
                    [both[:, :HALF], both[:, HALF:]], axis=0
                ).astype(bf16)
            part_copy(p, 0).start()

    def advance(members, s):
        for p in members:
            part_copy(p, s).wait_recv()
            half = come[s].shape[1]
            base = own_bit(orders[p][s]) * half
            if s < stages - 1:
                step = min(half, 4)

                @pl.loop(0, half // step)
                def _(i):
                    mine = held[s][p, pl.ds(base + i * step, step)].astype(f32)
                    theirs = come[s][p, pl.ds(i * step, step)].astype(f32)
                    held[s + 1][p, pl.ds(i * step, step)] = (mine + theirs).astype(bf16)

                part_copy(p, s + 1).start()
            else:
                mine = held[s][p, pl.ds(base, 1)].astype(f32)
                total = mine[0] + come[s][p, 0].astype(f32)
                rows = total.shape[0] // 2
                for i in range(2):
                    at = first_column(p) + i * HALF
                    value = total[i * rows:(i + 1) * rows]
                    if at < 3 * width:
                        gqkv_ref[:, at:at + HALF] = value
                    else:
                        gproj_ref[:, at - 3 * width:at - 3 * width + HALF] = value

    def advance_gain(s):
        gain_copy(s).wait_recv()
        total = gheld[s] + gcome[s]
        if s < stages - 1:
            gheld[s + 1] = total
            gain_copy(s + 1).start()
        else:
            gsum_ref[...] = total

    groups = HEADS // 4
    waves = [range(3 * i, 3 * i + 3) for i in range(parts // 3)]
    for group in range(groups):
        attention(group)
        if parts:
            open_parts(waves[group])
            for i in range(group):
                advance(waves[i], group - 1 - i)

    mixed_t[...] = mixed[...].T
    if parts:
        open_parts(waves[groups])
        for i in range(groups):
            advance(waves[i], groups - 1 - i)

    @pl.loop(0, width // COLS)
    def _(j):
        cols = pl.ds(pl.multiple_of(j * COLS, COLS), COLS)
        out = nn(mixed[...], wout_ref[:, cols])
        bg[:, cols] = (xs[:, cols].astype(f32) + out).astype(bf16)
        dnormed[:, cols] = nt(dpacked[...], wqkv_ref[cols, :]).astype(bf16)

    gheld[0] = jnp.zeros((8, width), f32)

    @pl.loop(0, windows)
    def _(w):
        rows = pl.ds(pl.multiple_of(w * WCAP, WCAP), WCAP)
        dn = dnormed[rows, :].astype(f32)
        u = unit[rows, :]
        gheld[0] += jnp.sum((dn * u).reshape(WCAP // 8, 8, width), axis=0)
        dunit = dn * gain_row
        dcentre = inv[rows, :] * (
            dunit
            - jnp.mean(dunit, axis=-1, keepdims=True)
            - u * jnp.mean(dunit * u, axis=-1, keepdims=True)
        )
        bg[rows, width:] = (xs[rows, width:].astype(f32) + dcentre).astype(bf16)

    gain_copy(0).start()
    received = (
        lax.broadcasted_iota(jnp.int32, (7 * cap, slots), 0) + count == wrow_ref[...]
    ).astype(f32).astype(bf16)
    for j in range(double // COLS):
        cols = slice(j * COLS, (j + 1) * COLS)
        ret[:, cols] = nn(received, bg[:, cols]).astype(bf16)
    for k in (6, 5, 4, 3, 2, 1, 0):
        @pl.when(found[k][3])
        def _():
            return_copy(k).start()
    kept = (
        lax.broadcasted_iota(jnp.int32, (count, slots), 0) == wrow_ref[...]
    ).astype(f32).astype(bf16)
    for j in range(double // COLS):
        cols = slice(j * COLS, (j + 1) * COLS)
        own_ref[:, cols] = nn(kept, bg[:, cols]).astype(bf16)

    if not parts:
        for j in range(4 * width // COLS):
            grad_ref[:, j * COLS:(j + 1) * COLS] = gradient(j * COLS)
    for turn in range(groups, stages + groups):
        for i in range(len(waves)):
            if 0 <= turn - i < stages:
                advance(waves[i], turn - i)
        if turn - groups < stages:
            advance_gain(turn - groups)

    for k in range(7):
        @pl.when(found[k][2])
        def _():
            return_copy(k).wait_recv()

        @pl.when(found[k][3])
        def _():
            return_copy(k).wait_send()
    for s in range(stages):
        for p in range(parts):
            part_copy(p, s).wait_send()
        gain_copy(s).wait_send()


def finish_kernel(own_ref, back_ref, place_ref, *refs):
    many = len(refs) // 2 - 1
    given, (block_ref, gtok_ref, *final) = refs[:many], refs[many:]
    width = block_ref.shape[1]
    place = place_ref[...]
    block_ref[...] = (
        own_ref[:, :width].astype(f32) + nn(place, back_ref[:, :width])
    ).astype(bf16)
    gtok_ref[...] = (
        own_ref[:, width:].astype(f32) + nn(place, back_ref[:, width:])
    ).astype(bf16)
    for source, target in zip(given, final):
        target[...] = source[...]


def on_device(sizes, tokens, norm_gain, w_qkv, w_out, send_rows, window_rows, grad_out):
    count, width = tokens.shape
    slots = window_rows.shape[1]
    cap = send_rows.shape[2]
    span = count + 7 * cap
    devices = sizes[0] * sizes[1] * sizes[2]
    vmem = pl.BlockSpec(memory_space=pltpu.VMEM)
    params = functools.partial(pltpu.CompilerParams, vmem_limit_bytes=VMEM_BYTES)

    by_axis = [[(a, 1 << i) for i in range(sizes[a].bit_length() - 1)] for a in range(3)]
    x_bits, y_bits, z_bits = by_axis
    bits = y_bits + x_bits + z_bits
    chunk = width // devices
    grouped = (
        all(1 << len(b) == n for b, n in zip(by_axis, sizes))
        and len(y_bits) > 0
        and chunk * devices == width
        and chunk % 8 == 0
    )
    parts = 4 * width // COLS
    orders, places = [], None
    if grouped:
        rest = y_bits[1:]
        kinds = [
            y_bits[:1] + x_bits + rest + z_bits,
            y_bits[:1] + rest + z_bits + x_bits,
            y_bits[:1] + z_bits + x_bits + rest,
        ]
        orders = [kinds[p % 3] for p in range(parts)]

        def position(order, c):
            at = (c // (sizes[1] * sizes[2]), c // sizes[2] % sizes[1], c % sizes[2])
            value = 0
            for axis, distance in order:
                value = 2 * value + at[axis] // distance % 2
            return value

        places = [[position(order, c) for c in range(devices)] for order in orders]

    stages = len(bits)
    anywhere = pl.BlockSpec(memory_space=pl.ANY)
    out_shape = [
        jax.ShapeDtypeStruct((count, 2 * width), bf16),
        jax.ShapeDtypeStruct((7 * cap, 2 * width), bf16),
        jax.ShapeDtypeStruct((count, 7 * cap), bf16),
        jax.ShapeDtypeStruct((8, width), f32),
    ]
    if grouped:
        sums = [
            jax.ShapeDtypeStruct((chunk, 3 * width), f32),
            jax.ShapeDtypeStruct((chunk, width), f32),
        ]
    else:
        sums = [jax.ShapeDtypeStruct((width, 4 * width), f32)]
    scratch = [
        pltpu.VMEM((7 * cap, 2 * width), bf16),
        pltpu.VMEM((span, 2 * width), bf16),
        pltpu.VMEM((width, 3 * width), bf16),
        pltpu.VMEM((width, width), bf16),
        pltpu.VMEM((slots, 1), jnp.int32),
        pltpu.VMEM((slots, span), bf16),
        pltpu.VMEM((slots, 2 * width), bf16),
        pltpu.VMEM((slots, width), f32),
        pltpu.VMEM((slots, width), bf16),
        pltpu.VMEM((width, slots), bf16),
        pltpu.VMEM((slots, 1), f32),
        pltpu.VMEM((slots, 3 * width), bf16),
        pltpu.VMEM((slots, width), bf16),
        pltpu.VMEM((slots, width), bf16),
        pltpu.VMEM((width, slots), bf16),
        pltpu.VMEM((slots, 3 * width), bf16),
        pltpu.VMEM((slots, width), bf16),
        pltpu.VMEM((slots, 2 * width), bf16),
        pltpu.VMEM((7 * cap, 2 * width), bf16),
        pltpu.VMEM((stages, 8, width), f32),
        pltpu.VMEM((stages, 8, width), f32),
        pltpu.SemaphoreType.DMA((2,)),
        pltpu.SemaphoreType.DMA((7,)),
        pltpu.SemaphoreType.DMA((7,)),
        pltpu.SemaphoreType.DMA((7,)),
        pltpu.SemaphoreType.DMA((7,)),
        pltpu.SemaphoreType.DMA((stages,)),
        pltpu.SemaphoreType.DMA((stages,)),
    ]
    if grouped:
        slab = (2 * chunk, HALF)
        scratch += [pltpu.VMEM((2, width, COLS), f32)]
        scratch += [pltpu.SemaphoreType.DMA((parts * stages,))] * 2
        scratch += [pltpu.VMEM((parts, devices >> (s + 1)) + slab, bf16) for s in range(stages)]
        scratch += [pltpu.VMEM((parts, devices >> s) + slab, bf16) for s in range(stages)]
    own, back, place, gain_sum, *grads = pl.pallas_call(
        functools.partial(block_kernel, sizes, orders, bits, places),
        out_shape=tuple(out_shape + sums),
        in_specs=[vmem] * 5 + [anywhere] * 2,
        out_specs=(vmem,) * len(out_shape + sums),
        scratch_shapes=scratch,
        compiler_params=params(collective_id=0, has_side_effects=True),
        name="block",
    )(tokens, grad_out, send_rows, window_rows, norm_gain, w_qkv, w_out)

    passed = grads if grouped else []
    final_shape = [jax.ShapeDtypeStruct((count, width), bf16)] * 2 + (sums if grouped else [])
    block_out, grad_tokens, *final = pl.pallas_call(
        finish_kernel,
        out_shape=tuple(final_shape),
        in_specs=[vmem] * (3 + len(passed)),
        out_specs=(vmem,) * len(final_shape),
        compiler_params=params(),
        name="finish",
    )(own, back, place, *passed)
    me = (lax.axis_index("gx") * sizes[1] + lax.axis_index("gy")) * sizes[2] + lax.axis_index("gz")
    grad_gain = jnp.sum(lax.dynamic_slice_in_dim(gain_sum, me * chunk, chunk, axis=1), axis=0)
    if grouped:
        grad_qkv, grad_proj = final
    else:
        summed = lax.psum_scatter(grads[0], AXES, scatter_dimension=0, tiled=True)
        grad_qkv, grad_proj = summed[:, :3 * width], summed[:, 3 * width:]
    return (block_out, grad_tokens, grad_gain, grad_qkv, grad_proj)


def solution(mesh):
    sizes = tuple(mesh.shape[a] for a in AXES)
    in_specs = (
        P(AXES, None),
        P(),
        P(),
        P(),
        P(AXES, None, None),
        P(AXES, None),
        P(AXES, None),
    )
    out_specs = (
        P(AXES, None),
        P(AXES, None),
        P(AXES),
        P(AXES, None),
        P(AXES, None),
    )
    return jax.shard_map(
        functools.partial(on_device, sizes),
        mesh=mesh,
        in_specs=in_specs,
        out_specs=out_specs,
        check_vma=False,
    )
```

time: 101 us -> 86.7 us (0.86)
  local copies, waits for them, and re-layouts: 9.07 us -> 1.28 us
  Pallas kernels: 88.5 us -> 83.2 us
    pallas_call x3 -> x2, Pallas kernels: 88.5 us -> 83.2 us  [the longest x1 80.5 us: on_device(): pl.pallas_call(functools.partial(block_kernel, sizes, orders, bits, place...]
    unnamed x8 -> x1, local copies, waits for them, and re-layouts: 4.86 us -> 1.28 us
    reshape x2 -> x0, local copies, waits for them, and re-layouts: 2.8 us -> none  [the longest x1 1.53 us: on_device(): slot_col = window_rows.reshape(slots, 1)]
    another operation x2 -> x0, local copies, waits for them, and re-layouts: 1.41 us -> none  [the longest x1 0.77 us: on_device(): send_col = send_flat.reshape(7 * cap, 1)]
where the time goes in v2:
time: 86.7 us; the launch traced here: 86.4 us
  Pallas kernels  83.2 us (96%)
  other arithmetic  1.3 us (1%)
  local copies, waits for them, and re-layouts  1.28 us (1%)
    pallas_call x1, Pallas kernels, on_device(): pl.pallas_call(functools.partial(block_kernel, sizes, orders, bits, place...  80.5 us
    pallas_call x1, Pallas kernels, on_device(): pl.pallas_call(finish_kernel, out_shape=tuple(final_shape), in_specs=[vme...  2.7 us

profile of v2, /device:TPU:0, one launch (start us, length us, event | category | flops | bytes accessed | tf_op | source)
XLA Modules:
  0.0 86.4 jit_solution(7131868461283732556)
XLA Ops:
  0.6 1.3 %copy.12.refs_2_ = s32[1,7,32]{2,1,0:T(8,128)} copy(s32[1,7,32]{2,0,1:T(1,128)} %param.11) | data formatting | bytes 1792 | tf_op args[4]
  1.9 80.5 %block.1 = (bf16[256,1536]{1,0:T(8,128)(2,1)}, bf16[224,1536]{1,0:T(8,128)(2,1)}, bf16[256,224]{1,0:T(8,128)(2,1)}, f32[8,768]{1,0:T(8,128)}, f32[24,2304]{1,0:T(8,128)}, /*index=5*/f32[24,768]{1,0:T(8,128)}) custom-call(bf16[256,768]{1,0:T(8,128)(2,1)} %refs_0_.1, bf16[256,768]{1,0:T(8,128)(2,1)} %refs_1_.1, s32[1,7,32]{2,1,0:T(8,128)} %copy.12.refs_2_, ...), custom_call_target="tpu_custom_call" | custom-call | tf_op jit(solution)/shard_map/block/pallas_call | solution.py:516
  82.4 1.3 %dynamic-slice_reduce_fusion = f32[24]{0:T(128)} fusion(f32[8,768]{1,0:T(8,128)} %get-tuple-element.22, s32[]{:T(128)S(6)} %select_n.3), kind=kLoop, calls=%fused_computation | loop fusion | flops 168 | bytes 868 | tf_op jit(solution)/shard_map/reduce_sum | solution.py:537
  83.7 2.7 %finish.1 = (bf16[256,768]{1,0:T(8,128)(2,1)}, bf16[256,768]{1,0:T(8,128)(2,1)}, f32[24,2304]{1,0:T(8,128)}, f32[24,768]{1,0:T(8,128)}) custom-call(bf16[256,1536]{1,0:T(8,128)(2,1)} %get-tuple-element.15.own_ref, bf16[224,1536]{1,0:T(8,128)(2,1)} %get-tuple-element.16.back_ref, bf16[256,224]{1,0:T(8,128)(2,1)} %get-tuple-element.17.place_ref, ...), custom_call_target="tpu_custom_call" | custom-call | tf_op jit(solution)/shard_map/finish/pallas_call | solution.py:528

commit v3 on v2

--- a/solution.py
+++ b/solution.py
@@ -11,6 +11,7 @@
 WCAP = 128
 COLS = 256
 HALF = 128
+PLAN = (0, 1, 2, 0, 1, 0, 1, 0, 1, 2, 1, 0)
 VMEM_BYTES = 56 * 1024 * 1024
 
 epsilon = 1e-06
@@ -120,12 +121,12 @@
             here[i] + distance * (1 - 2 * own_bit(bit)) if i == axis else here[i] for i in range(3)
         )
 
-    def forward_copy(k):
+    def forward_copy(h, k):
         return pltpu.make_async_remote_copy(
-            src_ref=buf.at[pl.ds(k * cap, cap)],
-            dst_ref=table.at[pl.ds(count + k * cap, cap)],
-            send_sem=send_sem.at[k],
-            recv_sem=recv_sem.at[k],
+            src_ref=buf.at[h, pl.ds(k * cap, cap)],
+            dst_ref=table.at[h, pl.ds(k * cap, cap)],
+            send_sem=send_sem.at[7 * h + k],
+            recv_sem=recv_sem.at[7 * h + k],
             device_id=found[k][0],
             device_id_type=MESH,
         )
@@ -169,24 +170,38 @@
     for load in loads:
         load.start()
 
-    send_row = jnp.concatenate([send_ref[0, k:k + 1, :] for k in range(7)], axis=1)
+    send_row = jnp.concatenate([send_ref[k] for k in range(7)], axis=1)
     place = (
         lax.broadcasted_iota(jnp.int32, (count, 7 * cap), 0) == send_row
     ).astype(f32).astype(bf16)
     place_ref[...] = place
-    buf[:, :width] = tn(place, tok_ref[...]).astype(bf16)
-    buf[:, width:] = tn(place, gout_ref[...]).astype(bf16)
+    buf[0] = tn(place, tok_ref[...]).astype(bf16)
     greet(found, [partner(bit) for bit in bits])
-    for k in (6, 5, 4, 3, 2, 1, 0):
-        @pl.when(found[k][2])
-        def _():
-            forward_copy(k).start()
-    table[:count, :width] = tok_ref[...]
-    table[:count, width:] = gout_ref[...]
+
+    def start_forward(h):
+        for k in (6, 5, 4, 3, 2, 1, 0):
+            @pl.when(found[k][2])
+            def _():
+                forward_copy(h, k).start()
+
+    def wait_forward(h):
+        for k in range(7):
+            @pl.when(found[k][3])
+            def _():
+                forward_copy(h, k).wait_recv()
+
+            @pl.when(found[k][2])
+            def _():
+                forward_copy(h, k).wait_send()
+
+    start_forward(0)
+    buf[1] = tn(place, gout_ref[...]).astype(bf16)
+    start_forward(1)
     for k in range(7):
         @pl.when(jnp.logical_not(found[k][3]))
         def _():
-            table[pl.ds(count + k * cap, cap), :] = jnp.zeros((cap, double), bf16)
+            for h in range(2):
+                table[h, pl.ds(k * cap, cap), :] = jnp.zeros((cap, width), bf16)
 
         @pl.when(jnp.logical_not(found[k][2]))
         def _():
@@ -196,21 +211,25 @@
         lax.broadcasted_iota(jnp.int32, (slots, span), 1) == wcol[...]
     ).astype(f32).astype(bf16)
     gain_row = gain_ref[...].reshape(1, width)
+    for h, own in enumerate((tok_ref, gout_ref)):
+        @pl.loop(0, width // COLS)
+        def _(j):
+            cols = pl.ds(pl.multiple_of(j * COLS, COLS), COLS)
+            into = pl.ds(pl.multiple_of(h * width + j * COLS, COLS), COLS)
+            xs[:, into] = nn(pick[:, :count], own[:, cols]).astype(bf16)
     for load in loads:
         load.wait()
-    for k in range(7):
-        @pl.when(found[k][3])
-        def _():
-            forward_copy(k).wait_recv()
-
-        @pl.when(found[k][2])
-        def _():
-            forward_copy(k).wait_send()
-
-    @pl.loop(0, double // COLS)
-    def _(j):
-        cols = pl.ds(pl.multiple_of(j * COLS, COLS), COLS)
-        xs[:, cols] = nn(pick[...], table[:, cols]).astype(bf16)
+
+    def fill(h):
+        @pl.loop(0, width // COLS)
+        def _(j):
+            cols = pl.ds(pl.multiple_of(j * COLS, COLS), COLS)
+            into = pl.ds(pl.multiple_of(h * width + j * COLS, COLS), COLS)
+            come_in = nn(pick[:, count:], table[h, :, cols])
+            xs[:, into] = (xs[:, into].astype(f32) + come_in).astype(bf16)
+
+    wait_forward(0)
+    fill(0)
 
     @pl.loop(0, windows)
     def _(w):
@@ -230,48 +249,55 @@
         cols = pl.ds(pl.multiple_of(j * COLS, COLS), COLS)
         packed[:, cols] = nn(normed[...], wqkv_ref[:, cols]).astype(bf16)
 
+    wait_forward(1)
+    fill(1)
+
     @pl.loop(0, width // COLS)
     def _(j):
         cols = pl.ds(pl.multiple_of(j * COLS, COLS), COLS)
         delta[:, cols] = nt(xs[:, width:], wout_ref[cols, :]).astype(bf16)
 
     def attention(group):
-        @pl.loop(0, windows)
-        def _(w):
-            rows = pl.ds(pl.multiple_of(w * WCAP, WCAP), WCAP)
-            valid = (wcol[rows, :] >= 0)[None]
-            first = lax.broadcasted_iota(jnp.int32, (WCAP, pair), 1) < head_dim
-            none = jnp.zeros((WCAP, pair), bf16)
-
-            def split(t):
-                return jnp.concatenate(
-                    [jnp.where(first, t, none), jnp.where(first, none, t)], axis=0
-                )
-
-            def join(t):
-                return jnp.where(first, t[:WCAP], t[WCAP:])
-
-            for j in (2 * group, 2 * group + 1):
-                at = j * pair
-                q = packed[rows, at:at + pair]
-                k2 = split(packed[rows, width + at:width + at + pair])
-                v2 = split(packed[rows, 2 * width + at:2 * width + at + pair])
-                g = delta[rows, at:at + pair]
-                scores = nt(k2, q).reshape(2, WCAP, WCAP) * scale
-                scores = jnp.where(valid, scores, big_negative)
-                top = jnp.max(scores, axis=1, keepdims=True)
-                expo = jnp.exp(scores - top)
-                probs = expo * (1.0 / jnp.sum(expo, axis=1, keepdims=True))
-                weights = probs.reshape(2 * WCAP, WCAP).astype(bf16)
-                mixed[rows, at:at + pair] = tn(weights, v2).astype(bf16)
-                dweights = nt(v2, g).reshape(2, WCAP, WCAP)
-                total = jnp.sum(dweights * probs, axis=1, keepdims=True)
-                dscaled = (probs * (dweights - total) * scale).reshape(2 * WCAP, WCAP).astype(bf16)
-                dpacked[rows, at:at + pair] = tn(dscaled, k2).astype(bf16)
-                dpacked[rows, width + at:width + at + pair] = join(nn(dscaled, q)).astype(bf16)
-                dpacked[rows, 2 * width + at:2 * width + at + pair] = join(
-                    nn(weights, g)
-                ).astype(bf16)
+        @pl.loop(0, windows // 2)
+        def _(turn):
+            window(group, 2 * turn)
+            window(group, 2 * turn + 1)
+
+    def window(group, w):
+        rows = pl.ds(pl.multiple_of(w * WCAP, WCAP), WCAP)
+        valid = (wcol[rows, :] >= 0)[None]
+        first = lax.broadcasted_iota(jnp.int32, (WCAP, pair), 1) < head_dim
+        none = jnp.zeros((WCAP, pair), bf16)
+
+        def split(t):
+            return jnp.concatenate(
+                [jnp.where(first, t, none), jnp.where(first, none, t)], axis=0
+            )
+
+        def join(t):
+            return jnp.where(first, t[:WCAP], t[WCAP:])
+
+        for j in (2 * group, 2 * group + 1):
+            at = j * pair
+            q = packed[rows, at:at + pair]
+            k2 = split(packed[rows, width + at:width + at + pair])
+            v2 = split(packed[rows, 2 * width + at:2 * width + at + pair])
+            g = delta[rows, at:at + pair]
+            scores = nt(k2, q).reshape(2, WCAP, WCAP) * scale
+            scores = jnp.where(valid, scores, big_negative)
+            top = jnp.max(scores, axis=1, keepdims=True)
+            expo = jnp.exp(scores - top)
+            probs = expo * (1.0 / jnp.sum(expo, axis=1, keepdims=True))
+            weights = probs.reshape(2 * WCAP, WCAP).astype(bf16)
+            mixed[rows, at:at + pair] = tn(weights, v2).astype(bf16)
+            dweights = nt(v2, g).reshape(2, WCAP, WCAP)
+            total = jnp.sum(dweights * probs, axis=1, keepdims=True)
+            dscaled = (probs * (dweights - total) * scale).reshape(2 * WCAP, WCAP).astype(bf16)
+            dpacked[rows, at:at + pair] = tn(dscaled, k2).astype(bf16)
+            dpacked[rows, width + at:width + at + pair] = join(nn(dscaled, q)).astype(bf16)
+            dpacked[rows, 2 * width + at:2 * width + at + pair] = join(
+                nn(weights, g)
+            ).astype(bf16)
 
     def first_column(p):
         return (p % 3) * width + (p // 3) * COLS if p < parts - 3 else 3 * width + (p - parts + 3) * COLS
@@ -330,18 +356,26 @@
 
     groups = HEADS // 4
     waves = [range(3 * i, 3 * i + 3) for i in range(parts // 3)]
+    stage_of = {}
+
+    def open_wave(i):
+        if parts:
+            open_parts(waves[i])
+            turn()
+            stage_of[i] = 0
+
+    def turn():
+        for i in sorted(stage_of):
+            if stage_of[i] < stages:
+                advance(waves[i], stage_of[i])
+                stage_of[i] += 1
+
     for group in range(groups):
         attention(group)
-        if parts:
-            open_parts(waves[group])
-            for i in range(group):
-                advance(waves[i], group - 1 - i)
+        open_wave(group)
 
     mixed_t[...] = mixed[...].T
-    if parts:
-        open_parts(waves[groups])
-        for i in range(groups):
-            advance(waves[i], groups - 1 - i)
+    open_wave(groups)
 
     @pl.loop(0, width // COLS)
     def _(j):
@@ -350,6 +384,7 @@
         bg[:, cols] = (xs[:, cols].astype(f32) + out).astype(bf16)
         dnormed[:, cols] = nt(dpacked[...], wqkv_ref[cols, :]).astype(bf16)
 
+    turn()
     gheld[0] = jnp.zeros((8, width), f32)
 
     @pl.loop(0, windows)
@@ -377,6 +412,7 @@
         @pl.when(found[k][3])
         def _():
             return_copy(k).start()
+    turn()
     kept = (
         lax.broadcasted_iota(jnp.int32, (count, slots), 0) == wrow_ref[...]
     ).astype(f32).astype(bf16)
@@ -387,12 +423,9 @@
     if not parts:
         for j in range(4 * width // COLS):
             grad_ref[:, j * COLS:(j + 1) * COLS] = gradient(j * COLS)
-    for turn in range(groups, stages + groups):
-        for i in range(len(waves)):
-            if 0 <= turn - i < stages:
-                advance(waves[i], turn - i)
-        if turn - groups < stages:
-            advance_gain(turn - groups)
+    for s in range(stages):
+        turn()
+        advance_gain(s)
 
     for k in range(7):
         @pl.when(found[k][2])
@@ -408,10 +441,11 @@
         gain_copy(s).wait_send()
 
 
-def finish_kernel(own_ref, back_ref, place_ref, *refs):
+def finish_kernel(sizes, own_ref, back_ref, place_ref, gsum_ref, *refs):
     many = len(refs) // 2 - 1
-    given, (block_ref, gtok_ref, *final) = refs[:many], refs[many:]
+    given, (block_ref, gtok_ref, gain_ref, *final) = refs[:many], refs[many:]
     width = block_ref.shape[1]
+    chunk = gain_ref.shape[1]
     place = place_ref[...]
     block_ref[...] = (
         own_ref[:, :width].astype(f32) + nn(place, back_ref[:, :width])
@@ -419,6 +453,9 @@
     gtok_ref[...] = (
         own_ref[:, width:].astype(f32) + nn(place, back_ref[:, width:])
     ).astype(bf16)
+    me = (lax.axis_index("gx") * sizes[1] + lax.axis_index("gy")) * sizes[2] + lax.axis_index("gz")
+    rolled = pltpu.roll(gsum_ref[...], lax.rem(width - me * chunk, width), 1)
+    gain_ref[...] = jnp.sum(rolled, axis=0, keepdims=True)[:, :chunk]
     for source, target in zip(given, final):
         target[...] = source[...]
 
@@ -448,10 +485,10 @@
         rest = y_bits[1:]
         kinds = [
             y_bits[:1] + x_bits + rest + z_bits,
-            y_bits[:1] + rest + z_bits + x_bits,
+            y_bits[:1] + rest + x_bits + z_bits,
             y_bits[:1] + z_bits + x_bits + rest,
         ]
-        orders = [kinds[p % 3] for p in range(parts)]
+        orders = [kinds[PLAN[p % len(PLAN)]] for p in range(parts)]
 
         def position(order, c):
             at = (c // (sizes[1] * sizes[2]), c // sizes[2] % sizes[1], c % sizes[2])
@@ -478,8 +515,8 @@
     else:
         sums = [jax.ShapeDtypeStruct((width, 4 * width), f32)]
     scratch = [
-        pltpu.VMEM((7 * cap, 2 * width), bf16),
-        pltpu.VMEM((span, 2 * width), bf16),
+        pltpu.VMEM((2, 7 * cap, width), bf16),
+        pltpu.VMEM((2, 7 * cap, width), bf16),
         pltpu.VMEM((width, 3 * width), bf16),
         pltpu.VMEM((width, width), bf16),
         pltpu.VMEM((slots, 1), jnp.int32),
@@ -500,8 +537,8 @@
         pltpu.VMEM((stages, 8, width), f32),
         pltpu.VMEM((stages, 8, width), f32),
         pltpu.SemaphoreType.DMA((2,)),
-        pltpu.SemaphoreType.DMA((7,)),
-        pltpu.SemaphoreType.DMA((7,)),
+        pltpu.SemaphoreType.DMA((14,)),
+        pltpu.SemaphoreType.DMA((14,)),
         pltpu.SemaphoreType.DMA((7,)),
         pltpu.SemaphoreType.DMA((7,)),
         pltpu.SemaphoreType.DMA((stages,)),
@@ -521,26 +558,25 @@
         scratch_shapes=scratch,
         compiler_params=params(collective_id=0, has_side_effects=True),
         name="block",
-    )(tokens, grad_out, send_rows, window_rows, norm_gain, w_qkv, w_out)
+    )(tokens, grad_out, jnp.transpose(send_rows, (1, 0, 2)), window_rows, norm_gain, w_qkv, w_out)
 
     passed = grads if grouped else []
-    final_shape = [jax.ShapeDtypeStruct((count, width), bf16)] * 2 + (sums if grouped else [])
-    block_out, grad_tokens, *final = pl.pallas_call(
-        finish_kernel,
+    final_shape = [jax.ShapeDtypeStruct((count, width), bf16)] * 2
+    final_shape += [jax.ShapeDtypeStruct((1, chunk), f32)] + (sums if grouped else [])
+    block_out, grad_tokens, grad_gain, *final = pl.pallas_call(
+        functools.partial(finish_kernel, sizes),
         out_shape=tuple(final_shape),
-        in_specs=[vmem] * (3 + len(passed)),
+        in_specs=[vmem] * (4 + len(passed)),
         out_specs=(vmem,) * len(final_shape),
         compiler_params=params(),
         name="finish",
-    )(own, back, place, *passed)
-    me = (lax.axis_index("gx") * sizes[1] + lax.axis_index("gy")) * sizes[2] + lax.axis_index("gz")
-    grad_gain = jnp.sum(lax.dynamic_slice_in_dim(gain_sum, me * chunk, chunk, axis=1), axis=0)
+    )(own, back, place, gain_sum, *passed)
     if grouped:
         grad_qkv, grad_proj = final
     else:
         summed = lax.psum_scatter(grads[0], AXES, scatter_dimension=0, tiled=True)
         grad_qkv, grad_proj = summed[:, :3 * width], summed[:, 3 * width:]
-    return (block_out, grad_tokens, grad_gain, grad_qkv, grad_proj)
+    return (block_out, grad_tokens, grad_gain.reshape(chunk), grad_qkv, grad_proj)
 
 
 def solution(mesh):

time: 86.7 us -> 82.8 us (0.955)
  Pallas kernels: 83.2 us -> 81.5 us
  other arithmetic: 1.3 us -> 0 us
  local copies, waits for them, and re-layouts: 1.28 us -> 0 us
    pallas_call x1, Pallas kernels: 80.5 us -> 78.8 us  [on_device(): pl.pallas_call(functools.partial(block_kernel, sizes, orders, bits, place...]
    reduce_sum x1 -> x0, other arithmetic: 1.3 us -> none  [on_device(): jnp.sum(lax.dynamic_slice_in_dim(gain_sum, me * chunk, chunk, axis=1), ax...]
    unnamed x1 -> x0, local copies, waits for them, and re-layouts: 1.28 us -> none
where the time goes in v3:
time: 82.8 us; the launch traced here: 82.1 us
  Pallas kernels  81.5 us (98%)
    pallas_call x1, Pallas kernels, on_device(): pl.pallas_call(functools.partial(block_kernel, sizes, orders, bits, place...  78.8 us
    pallas_call x1, Pallas kernels, on_device(): pl.pallas_call(functools.partial(finish_kernel, sizes), out_shape=tuple(f...  2.72 us

profile of v3, /device:TPU:0, one launch (start us, length us, event | category | flops | bytes accessed | tf_op | source)
XLA Modules:
  0.0 82.1 jit_solution(12270381191251358302)
XLA Ops:
  0.6 78.8 %block.1 = (bf16[256,1536]{1,0:T(8,128)(2,1)}, bf16[224,1536]{1,0:T(8,128)(2,1)}, bf16[256,224]{1,0:T(8,128)(2,1)}, f32[8,768]{1,0:T(8,128)}, f32[24,2304]{1,0:T(8,128)}, /*index=5*/f32[24,768]{1,0:T(8,128)}) custom-call(bf16[256,768]{1,0:T(8,128)(2,1)} %refs_0_.1, bf16[256,768]{1,0:T(8,128)(2,1)} %refs_1_.1, s32[7,1,32]{2,1,0:T(1,128)} %bitcast.2, ...), custom_call_target="tpu_custom_call" | custom-call | tf_op jit(solution)/shard_map/block/pallas_call | solution.py:553
  79.4 2.7 %finish.1 = (bf16[256,768]{1,0:T(8,128)(2,1)}, bf16[256,768]{1,0:T(8,128)(2,1)}, f32[1,24]{1,0:T(1,128)}, f32[24,2304]{1,0:T(8,128)}, f32[24,768]{1,0:T(8,128)}) custom-call(bf16[256,1536]{1,0:T(8,128)(2,1)} %get-tuple-element.16.own_ref, bf16[224,1536]{1,0:T(8,128)(2,1)} %get-tuple-element.17.back_ref, bf16[256,224]{1,0:T(8,128)(2,1)} %get-tuple-element.18.place_ref, ...), custom_call_target="tpu_custom_call" | custom-call | tf_op jit(solution)/shard_map/finish/pallas_call | solution.py:566

commit v4 on v3

--- a/solution.py
+++ b/solution.py
@@ -11,7 +11,6 @@
 WCAP = 128
 COLS = 256
 HALF = 128
-PLAN = (0, 1, 2, 0, 1, 0, 1, 0, 1, 2, 1, 0)
 VMEM_BYTES = 56 * 1024 * 1024
 
 epsilon = 1e-06
@@ -75,7 +74,9 @@
 
 
 def block_kernel(sizes, orders, bits, places, *refs):
-    parts, stages = len(orders), len(bits)
+    parts, pairs = len(orders), len(bits)
+    stages = pairs + 1
+    deep = sizes[2]
     refs = list(refs)
 
     def take(n):
@@ -91,12 +92,13 @@
         (grad_ref,) = take(1)
     buf, table, wqkv_ref, wout_ref, wcol, pick = take(6)
     xs, unit, normed, normed_t, inv, packed, delta, mixed, mixed_t, dpacked, dnormed = take(11)
-    bg, ret = take(2)
-    gheld, gcome = take(2)
+    bg, ret, held_probs = take(3)
+    gheld, gcome, gcome_z = take(3)
     load_sem, send_sem, recv_sem, ret_send, ret_recv, gain_send, gain_recv = take(7)
+    gain_send_z, gain_recv_z = take(2)
     if parts:
-        piece, part_send, part_recv = take(3)
-        come = take(stages)
+        piece, part_send, part_recv, send_z, recv_z, come_z = take(6)
+        come = take(pairs)
         held = take(stages)
 
     found = neighbours(sizes)
@@ -131,13 +133,36 @@
             device_id_type=MESH,
         )
 
-    def return_copy(k):
+    def along_z(d):
+        return (here[0], here[1], lax.rem(here[2] + d, deep))
+
+    def return_copy(h, k):
         return pltpu.make_async_remote_copy(
-            src_ref=ret.at[pl.ds(k * cap, cap)],
-            dst_ref=back_ref.at[pl.ds(k * cap, cap)],
-            send_sem=ret_send.at[k],
-            recv_sem=ret_recv.at[k],
+            src_ref=ret.at[h, pl.ds(k * cap, cap)],
+            dst_ref=back_ref.at[h, pl.ds(k * cap, cap)],
+            send_sem=ret_send.at[7 * h + k],
+            recv_sem=ret_recv.at[7 * h + k],
             device_id=found[k][1],
+            device_id_type=MESH,
+        )
+
+    def part_copy_z(p, d):
+        return pltpu.make_async_remote_copy(
+            src_ref=held[pairs].at[p, pl.ds(along_z(d)[2], 1)],
+            dst_ref=come_z.at[p, pl.ds(d - 1, 1)],
+            send_sem=send_z.at[p * (deep - 1) + d - 1],
+            recv_sem=recv_z.at[p * (deep - 1) + d - 1],
+            device_id=along_z(d),
+            device_id_type=MESH,
+        )
+
+    def gain_copy_z(d):
+        return pltpu.make_async_remote_copy(
+            src_ref=gheld.at[pairs],
+            dst_ref=gcome_z.at[d - 1],
+            send_sem=gain_send_z.at[d - 1],
+            recv_sem=gain_recv_z.at[d - 1],
+            device_id=along_z(d),
             device_id_type=MESH,
         )
 
@@ -147,8 +172,8 @@
         return pltpu.make_async_remote_copy(
             src_ref=held[s].at[p, pl.ds((1 - own_bit(bit)) * half, half)],
             dst_ref=come[s].at[p],
-            send_sem=part_send.at[p * stages + s],
-            recv_sem=part_recv.at[p * stages + s],
+            send_sem=part_send.at[p * pairs + s],
+            recv_sem=part_recv.at[p * pairs + s],
             device_id=partner(bit),
             device_id_type=MESH,
         )
@@ -176,7 +201,7 @@
     ).astype(f32).astype(bf16)
     place_ref[...] = place
     buf[0] = tn(place, tok_ref[...]).astype(bf16)
-    greet(found, [partner(bit) for bit in bits])
+    greet(found, [partner(bit) for bit in bits] + [along_z(d) for d in range(1, deep)])
 
     def start_forward(h):
         for k in (6, 5, 4, 3, 2, 1, 0):
@@ -189,10 +214,6 @@
             @pl.when(found[k][3])
             def _():
                 forward_copy(h, k).wait_recv()
-
-            @pl.when(found[k][2])
-            def _():
-                forward_copy(h, k).wait_send()
 
     start_forward(0)
     buf[1] = tn(place, gout_ref[...]).astype(bf16)
@@ -205,7 +226,8 @@
 
         @pl.when(jnp.logical_not(found[k][2]))
         def _():
-            back_ref[pl.ds(k * cap, cap), :] = jnp.zeros((cap, double), bf16)
+            for h in range(2):
+                back_ref[h, pl.ds(k * cap, cap), :] = jnp.zeros((cap, width), bf16)
     wcol[...] = jnp.broadcast_to(wrow_ref[...], (8, slots)).T[:, :1]
     pick[...] = (
         lax.broadcasted_iota(jnp.int32, (slots, span), 1) == wcol[...]
@@ -249,6 +271,88 @@
         cols = pl.ds(pl.multiple_of(j * COLS, COLS), COLS)
         packed[:, cols] = nn(normed[...], wqkv_ref[:, cols]).astype(bf16)
 
+    first = lax.broadcasted_iota(jnp.int32, (WCAP, pair), 1) < head_dim
+    none = jnp.zeros((WCAP, pair), bf16)
+
+    def split(t):
+        return jnp.concatenate([jnp.where(first, t, none), jnp.where(first, none, t)], axis=0)
+
+    def join(t):
+        return jnp.where(first, t[:WCAP], t[WCAP:])
+
+    def both_heads(w):
+        return pl.ds(pl.multiple_of(w * 2 * WCAP, 2 * WCAP), 2 * WCAP)
+
+    def forward(w, j, valid):
+        rows = pl.ds(pl.multiple_of(w * WCAP, WCAP), WCAP)
+        at = j * pair
+        q = packed[rows, at:at + pair]
+        k2 = split(packed[rows, width + at:width + at + pair])
+        v2 = split(packed[rows, 2 * width + at:2 * width + at + pair])
+        scores = nt(k2, q).reshape(2, WCAP, WCAP) * scale
+        scores = jnp.where(valid, scores, big_negative)
+        top = jnp.max(scores, axis=1, keepdims=True)
+        expo = jnp.exp(scores - top)
+        probs = expo * (1.0 / jnp.sum(expo, axis=1, keepdims=True))
+        probs = probs.reshape(2 * WCAP, WCAP)
+        held_probs[j, both_heads(w), :] = probs
+        mixed[rows, at:at + pair] = tn(probs.astype(bf16), v2).astype(bf16)
+
+    def backward(w, j):
+        rows = pl.ds(pl.multiple_of(w * WCAP, WCAP), WCAP)
+        at = j * pair
+        q = packed[rows, at:at + pair]
+        k2 = split(packed[rows, width + at:width + at + pair])
+        v2 = split(packed[rows, 2 * width + at:2 * width + at + pair])
+        g = delta[rows, at:at + pair]
+        probs = held_probs[j, both_heads(w), :]
+        weights = probs.astype(bf16)
+        probs = probs.reshape(2, WCAP, WCAP)
+        dweights = nt(v2, g).reshape(2, WCAP, WCAP)
+        total = jnp.sum(dweights * probs, axis=1, keepdims=True)
+        dscaled = (probs * (dweights - total) * scale).reshape(2 * WCAP, WCAP).astype(bf16)
+        dpacked[rows, at:at + pair] = tn(dscaled, k2).astype(bf16)
+        dpacked[rows, width + at:width + at + pair] = join(nn(dscaled, q)).astype(bf16)
+        dpacked[rows, 2 * width + at:2 * width + at + pair] = join(nn(weights, g)).astype(bf16)
+
+    def backward_group(group):
+        @pl.loop(0, windows // 2)
+        def _(i):
+            for w in (2 * i, 2 * i + 1):
+                for j in (2 * group, 2 * group + 1):
+                    backward(w, j)
+
+    @pl.loop(0, windows)
+    def _(w):
+        valid = (wcol[pl.ds(pl.multiple_of(w * WCAP, WCAP), WCAP), :] >= 0)[None]
+        for j in range(HEADS // 2):
+            forward(w, j, valid)
+
+    @pl.loop(0, width // COLS)
+    def _(j):
+        cols = pl.ds(pl.multiple_of(j * COLS, COLS), COLS)
+        out = nn(mixed[...], wout_ref[:, cols])
+        bg[:, cols] = (xs[:, cols].astype(f32) + out).astype(bf16)
+
+    received = (
+        lax.broadcasted_iota(jnp.int32, (7 * cap, slots), 0) + count == wrow_ref[...]
+    ).astype(f32).astype(bf16)
+
+    def collect_returns(h):
+        for j in range(width // COLS):
+            cols = slice(j * COLS, (j + 1) * COLS)
+            into = slice(h * width + j * COLS, h * width + (j + 1) * COLS)
+            ret[h, :, cols] = nn(received, bg[:, into]).astype(bf16)
+
+    def start_returns(h, members):
+        for k in members:
+            @pl.when(found[k][3])
+            def _():
+                return_copy(h, k).start()
+
+    collect_returns(0)
+    start_returns(0, (6, 5, 4, 3, 2, 1, 0))
+
     wait_forward(1)
     fill(1)
 
@@ -257,50 +361,10 @@
         cols = pl.ds(pl.multiple_of(j * COLS, COLS), COLS)
         delta[:, cols] = nt(xs[:, width:], wout_ref[cols, :]).astype(bf16)
 
-    def attention(group):
-        @pl.loop(0, windows // 2)
-        def _(turn):
-            window(group, 2 * turn)
-            window(group, 2 * turn + 1)
-
-    def window(group, w):
-        rows = pl.ds(pl.multiple_of(w * WCAP, WCAP), WCAP)
-        valid = (wcol[rows, :] >= 0)[None]
-        first = lax.broadcasted_iota(jnp.int32, (WCAP, pair), 1) < head_dim
-        none = jnp.zeros((WCAP, pair), bf16)
-
-        def split(t):
-            return jnp.concatenate(
-                [jnp.where(first, t, none), jnp.where(first, none, t)], axis=0
-            )
-
-        def join(t):
-            return jnp.where(first, t[:WCAP], t[WCAP:])
-
-        for j in (2 * group, 2 * group + 1):
-            at = j * pair
-            q = packed[rows, at:at + pair]
-            k2 = split(packed[rows, width + at:width + at + pair])
-            v2 = split(packed[rows, 2 * width + at:2 * width + at + pair])
-            g = delta[rows, at:at + pair]
-            scores = nt(k2, q).reshape(2, WCAP, WCAP) * scale
-            scores = jnp.where(valid, scores, big_negative)
-            top = jnp.max(scores, axis=1, keepdims=True)
-            expo = jnp.exp(scores - top)
-            probs = expo * (1.0 / jnp.sum(expo, axis=1, keepdims=True))
-            weights = probs.reshape(2 * WCAP, WCAP).astype(bf16)
-            mixed[rows, at:at + pair] = tn(weights, v2).astype(bf16)
-            dweights = nt(v2, g).reshape(2, WCAP, WCAP)
-            total = jnp.sum(dweights * probs, axis=1, keepdims=True)
-            dscaled = (probs * (dweights - total) * scale).reshape(2 * WCAP, WCAP).astype(bf16)
-            dpacked[rows, at:at + pair] = tn(dscaled, k2).astype(bf16)
-            dpacked[rows, width + at:width + at + pair] = join(nn(dscaled, q)).astype(bf16)
-            dpacked[rows, 2 * width + at:2 * width + at + pair] = join(
-                nn(weights, g)
-            ).astype(bf16)
-
     def first_column(p):
-        return (p % 3) * width + (p // 3) * COLS if p < parts - 3 else 3 * width + (p - parts + 3) * COLS
+        if p < 3:
+            return 3 * width + p * COLS
+        return (p % 3) * width + (p // 3 - 1) * COLS
 
     def gradient(at):
         if at < 3 * width:
@@ -320,10 +384,10 @@
 
     def advance(members, s):
         for p in members:
-            part_copy(p, s).wait_recv()
-            half = come[s].shape[1]
-            base = own_bit(orders[p][s]) * half
-            if s < stages - 1:
+            if s < pairs:
+                part_copy(p, s).wait_recv()
+                half = come[s].shape[1]
+                base = own_bit(orders[p][s]) * half
                 step = min(half, 4)
 
                 @pl.loop(0, half // step)
@@ -332,10 +396,16 @@
                     theirs = come[s][p, pl.ds(i * step, step)].astype(f32)
                     held[s + 1][p, pl.ds(i * step, step)] = (mine + theirs).astype(bf16)
 
-                part_copy(p, s + 1).start()
+                if s + 1 < pairs:
+                    part_copy(p, s + 1).start()
+                else:
+                    for d in range(1, deep):
+                        part_copy_z(p, d).start()
             else:
-                mine = held[s][p, pl.ds(base, 1)].astype(f32)
-                total = mine[0] + come[s][p, 0].astype(f32)
+                total = held[s][p, pl.ds(here[2], 1)].astype(f32)[0]
+                for d in range(1, deep):
+                    part_copy_z(p, d).wait_recv()
+                    total = total + come_z[p, d - 1].astype(f32)
                 rows = total.shape[0] // 2
                 for i in range(2):
                     at = first_column(p) + i * HALF
@@ -346,12 +416,19 @@
                         gproj_ref[:, at - 3 * width:at - 3 * width + HALF] = value
 
     def advance_gain(s):
-        gain_copy(s).wait_recv()
-        total = gheld[s] + gcome[s]
-        if s < stages - 1:
-            gheld[s + 1] = total
-            gain_copy(s + 1).start()
+        if s < pairs:
+            gain_copy(s).wait_recv()
+            gheld[s + 1] = gheld[s] + gcome[s]
+            if s + 1 < pairs:
+                gain_copy(s + 1).start()
+            else:
+                for d in range(1, deep):
+                    gain_copy_z(d).start()
         else:
+            total = gheld[s]
+            for d in range(1, deep):
+                gain_copy_z(d).wait_recv()
+                total = total + gcome_z[d - 1]
             gsum_ref[...] = total
 
     groups = HEADS // 4
@@ -370,18 +447,15 @@
                 advance(waves[i], stage_of[i])
                 stage_of[i] += 1
 
+    mixed_t[...] = mixed[...].T
+    open_wave(0)
     for group in range(groups):
-        attention(group)
-        open_wave(group)
-
-    mixed_t[...] = mixed[...].T
-    open_wave(groups)
+        backward_group(group)
+        open_wave(group + 1)
 
     @pl.loop(0, width // COLS)
     def _(j):
         cols = pl.ds(pl.multiple_of(j * COLS, COLS), COLS)
-        out = nn(mixed[...], wout_ref[:, cols])
-        bg[:, cols] = (xs[:, cols].astype(f32) + out).astype(bf16)
         dnormed[:, cols] = nt(dpacked[...], wqkv_ref[cols, :]).astype(bf16)
 
     turn()
@@ -402,17 +476,11 @@
         bg[rows, width:] = (xs[rows, width:].astype(f32) + dcentre).astype(bf16)
 
     gain_copy(0).start()
-    received = (
-        lax.broadcasted_iota(jnp.int32, (7 * cap, slots), 0) + count == wrow_ref[...]
-    ).astype(f32).astype(bf16)
-    for j in range(double // COLS):
-        cols = slice(j * COLS, (j + 1) * COLS)
-        ret[:, cols] = nn(received, bg[:, cols]).astype(bf16)
-    for k in (6, 5, 4, 3, 2, 1, 0):
-        @pl.when(found[k][3])
-        def _():
-            return_copy(k).start()
+    collect_returns(1)
+    start_returns(1, (6, 5, 4, 3))
     turn()
+    advance_gain(0)
+    start_returns(1, (2, 1, 0))
     kept = (
         lax.broadcasted_iota(jnp.int32, (count, slots), 0) == wrow_ref[...]
     ).astype(f32).astype(bf16)
@@ -423,22 +491,28 @@
     if not parts:
         for j in range(4 * width // COLS):
             grad_ref[:, j * COLS:(j + 1) * COLS] = gradient(j * COLS)
-    for s in range(stages):
+    for s in range(1, stages):
         turn()
         advance_gain(s)
 
-    for k in range(7):
-        @pl.when(found[k][2])
-        def _():
-            return_copy(k).wait_recv()
-
-        @pl.when(found[k][3])
-        def _():
-            return_copy(k).wait_send()
-    for s in range(stages):
+    for h in range(2):
+        for k in range(7):
+            @pl.when(found[k][2])
+            def _():
+                return_copy(h, k).wait_recv()
+                forward_copy(h, k).wait_send()
+
+            @pl.when(found[k][3])
+            def _():
+                return_copy(h, k).wait_send()
+    for s in range(pairs):
         for p in range(parts):
             part_copy(p, s).wait_send()
         gain_copy(s).wait_send()
+    for d in range(1, deep):
+        for p in range(parts):
+            part_copy_z(p, d).wait_send()
+        gain_copy_z(d).wait_send()
 
 
 def finish_kernel(sizes, own_ref, back_ref, place_ref, gsum_ref, *refs):
@@ -448,10 +522,10 @@
     chunk = gain_ref.shape[1]
     place = place_ref[...]
     block_ref[...] = (
-        own_ref[:, :width].astype(f32) + nn(place, back_ref[:, :width])
+        own_ref[:, :width].astype(f32) + nn(place, back_ref[0])
     ).astype(bf16)
     gtok_ref[...] = (
-        own_ref[:, width:].astype(f32) + nn(place, back_ref[:, width:])
+        own_ref[:, width:].astype(f32) + nn(place, back_ref[1])
     ).astype(bf16)
     me = (lax.axis_index("gx") * sizes[1] + lax.axis_index("gy")) * sizes[2] + lax.axis_index("gz")
     rolled = pltpu.roll(gsum_ref[...], lax.rem(width - me * chunk, width), 1)
@@ -471,11 +545,12 @@
 
     by_axis = [[(a, 1 << i) for i in range(sizes[a].bit_length() - 1)] for a in range(3)]
     x_bits, y_bits, z_bits = by_axis
-    bits = y_bits + x_bits + z_bits
+    bits = y_bits + x_bits
     chunk = width // devices
     grouped = (
         all(1 << len(b) == n for b, n in zip(by_axis, sizes))
         and len(y_bits) > 0
+        and sizes[2] > 1
         and chunk * devices == width
         and chunk % 8 == 0
     )
@@ -483,27 +558,23 @@
     orders, places = [], None
     if grouped:
         rest = y_bits[1:]
-        kinds = [
-            y_bits[:1] + x_bits + rest + z_bits,
-            y_bits[:1] + rest + x_bits + z_bits,
-            y_bits[:1] + z_bits + x_bits + rest,
-        ]
-        orders = [kinds[PLAN[p % len(PLAN)]] for p in range(parts)]
+        kinds = [y_bits[:1] + x_bits + rest, y_bits[:1] + rest + x_bits]
+        orders = [kinds[p % 2] for p in range(parts)]
 
         def position(order, c):
             at = (c // (sizes[1] * sizes[2]), c // sizes[2] % sizes[1], c % sizes[2])
             value = 0
             for axis, distance in order:
                 value = 2 * value + at[axis] // distance % 2
-            return value
+            return value * sizes[2] + at[2]
 
         places = [[position(order, c) for c in range(devices)] for order in orders]
 
-    stages = len(bits)
+    pairs, deep = len(bits), sizes[2]
     anywhere = pl.BlockSpec(memory_space=pl.ANY)
     out_shape = [
         jax.ShapeDtypeStruct((count, 2 * width), bf16),
-        jax.ShapeDtypeStruct((7 * cap, 2 * width), bf16),
+        jax.ShapeDtypeStruct((2, 7 * cap, width), bf16),
         jax.ShapeDtypeStruct((count, 7 * cap), bf16),
         jax.ShapeDtypeStruct((8, width), f32),
     ]
@@ -533,23 +604,29 @@
         pltpu.VMEM((slots, 3 * width), bf16),
         pltpu.VMEM((slots, width), bf16),
         pltpu.VMEM((slots, 2 * width), bf16),
-        pltpu.VMEM((7 * cap, 2 * width), bf16),
-        pltpu.VMEM((stages, 8, width), f32),
-        pltpu.VMEM((stages, 8, width), f32),
+        pltpu.VMEM((2, 7 * cap, width), bf16),
+        pltpu.VMEM((HEADS // 2, 2 * slots, WCAP), f32),
+        pltpu.VMEM((pairs + 1, 8, width), f32),
+        pltpu.VMEM((pairs, 8, width), f32),
+        pltpu.VMEM((deep - 1, 8, width), f32),
         pltpu.SemaphoreType.DMA((2,)),
         pltpu.SemaphoreType.DMA((14,)),
         pltpu.SemaphoreType.DMA((14,)),
-        pltpu.SemaphoreType.DMA((7,)),
-        pltpu.SemaphoreType.DMA((7,)),
-        pltpu.SemaphoreType.DMA((stages,)),
-        pltpu.SemaphoreType.DMA((stages,)),
+        pltpu.SemaphoreType.DMA((14,)),
+        pltpu.SemaphoreType.DMA((14,)),
+        pltpu.SemaphoreType.DMA((pairs,)),
+        pltpu.SemaphoreType.DMA((pairs,)),
+        pltpu.SemaphoreType.DMA((deep - 1,)),
+        pltpu.SemaphoreType.DMA((deep - 1,)),
     ]
     if grouped:
         slab = (2 * chunk, HALF)
         scratch += [pltpu.VMEM((2, width, COLS), f32)]
-        scratch += [pltpu.SemaphoreType.DMA((parts * stages,))] * 2
-        scratch += [pltpu.VMEM((parts, devices >> (s + 1)) + slab, bf16) for s in range(stages)]
-        scratch += [pltpu.VMEM((parts, devices >> s) + slab, bf16) for s in range(stages)]
+        scratch += [pltpu.SemaphoreType.DMA((parts * pairs,))] * 2
+        scratch += [pltpu.SemaphoreType.DMA((parts * (deep - 1),))] * 2
+        scratch += [pltpu.VMEM((parts, deep - 1) + slab, bf16)]
+        scratch += [pltpu.VMEM((parts, devices >> (s + 1)) + slab, bf16) for s in range(pairs)]
+        scratch += [pltpu.VMEM((parts, devices >> s) + slab, bf16) for s in range(pairs + 1)]
     own, back, place, gain_sum, *grads = pl.pallas_call(
         functools.partial(block_kernel, sizes, orders, bits, places),
         out_shape=tuple(out_shape + sums),

time: 82.8 us -> 76.3 us (0.921)
  Pallas kernels: 81.5 us -> 75.4 us
    pallas_call x1, Pallas kernels: 78.8 us -> 72.7 us  [on_device(): pl.pallas_call(functools.partial(block_kernel, sizes, orders, bits, place...]
where the time goes in v4:
time: 76.3 us; the launch traced here: 76.1 us
  Pallas kernels  75.4 us (99%)
    pallas_call x1, Pallas kernels, on_device(): pl.pallas_call(functools.partial(block_kernel, sizes, orders, bits, place...  72.7 us
    pallas_call x1, Pallas kernels, on_device(): pl.pallas_call(functools.partial(finish_kernel, sizes), out_shape=tuple(f...  2.73 us

profile of v4, /device:TPU:0, one launch (start us, length us, event | category | flops | bytes accessed | tf_op | source)
XLA Modules:
  0.0 76.1 jit_solution(8327168671875065181)
XLA Ops:
  0.6 72.7 %block.1 = (bf16[256,1536]{1,0:T(8,128)(2,1)}, bf16[2,224,768]{2,1,0:T(8,128)(2,1)}, bf16[256,224]{1,0:T(8,128)(2,1)}, f32[8,768]{1,0:T(8,128)}, f32[24,2304]{1,0:T(8,128)}, /*index=5*/f32[24,768]{1,0:T(8,128)}) custom-call(bf16[256,768]{1,0:T(8,128)(2,1)} %refs_0_.1, bf16[256,768]{1,0:T(8,128)(2,1)} %refs_1_.1, s32[7,1,32]{2,1,0:T(1,128)} %bitcast.2, ...), custom_call_target="tpu_custom_call" | custom-call | tf_op jit(solution)/shard_map/block/pallas_call | solution.py:630
  73.4 2.7 %finish.1 = (bf16[256,768]{1,0:T(8,128)(2,1)}, bf16[256,768]{1,0:T(8,128)(2,1)}, f32[1,24]{1,0:T(1,128)}, f32[24,2304]{1,0:T(8,128)}, f32[24,768]{1,0:T(8,128)}) custom-call(bf16[256,1536]{1,0:T(8,128)(2,1)} %get-tuple-element.16.own_ref, bf16[2,224,768]{2,1,0:T(8,128)(2,1)} %get-tuple-element.17.back_ref, bf16[256,224]{1,0:T(8,128)(2,1)} %get-tuple-element.18.place_ref, ...), custom_call_target="tpu_custom_call" | custom-call | tf_op jit(solution)/shard_map/finish/pallas_call | solution.py:643

commit v5 on v4

--- a/solution.py
+++ b/solution.py
@@ -234,7 +234,7 @@
     ).astype(f32).astype(bf16)
     gain_row = gain_ref[...].reshape(1, width)
     for h, own in enumerate((tok_ref, gout_ref)):
-        @pl.loop(0, width // COLS)
+        @pl.loop(0, width // COLS, unroll=True)
         def _(j):
             cols = pl.ds(pl.multiple_of(j * COLS, COLS), COLS)
             into = pl.ds(pl.multiple_of(h * width + j * COLS, COLS), COLS)
@@ -243,7 +243,7 @@
         load.wait()
 
     def fill(h):
-        @pl.loop(0, width // COLS)
+        @pl.loop(0, width // COLS, unroll=True)
         def _(j):
             cols = pl.ds(pl.multiple_of(j * COLS, COLS), COLS)
             into = pl.ds(pl.multiple_of(h * width + j * COLS, COLS), COLS)
@@ -253,7 +253,7 @@
     wait_forward(0)
     fill(0)
 
-    @pl.loop(0, windows)
+    @pl.loop(0, windows, unroll=2)
     def _(w):
         rows = pl.ds(pl.multiple_of(w * WCAP, WCAP), WCAP)
         floats = xs[rows, :width].astype(f32)
@@ -266,7 +266,7 @@
 
     normed_t[...] = normed[...].T
 
-    @pl.loop(0, 3 * width // COLS)
+    @pl.loop(0, 3 * width // COLS, unroll=3)
     def _(j):
         cols = pl.ds(pl.multiple_of(j * COLS, COLS), COLS)
         packed[:, cols] = nn(normed[...], wqkv_ref[:, cols]).astype(bf16)
@@ -328,7 +328,7 @@
         for j in range(HEADS // 2):
             forward(w, j, valid)
 
-    @pl.loop(0, width // COLS)
+    @pl.loop(0, width // COLS, unroll=True)
     def _(j):
         cols = pl.ds(pl.multiple_of(j * COLS, COLS), COLS)
         out = nn(mixed[...], wout_ref[:, cols])
@@ -356,7 +356,7 @@
     wait_forward(1)
     fill(1)
 
-    @pl.loop(0, width // COLS)
+    @pl.loop(0, width // COLS, unroll=True)
     def _(j):
         cols = pl.ds(pl.multiple_of(j * COLS, COLS), COLS)
         delta[:, cols] = nt(xs[:, width:], wout_ref[cols, :]).astype(bf16)
@@ -453,7 +453,7 @@
         backward_group(group)
         open_wave(group + 1)
 
-    @pl.loop(0, width // COLS)
+    @pl.loop(0, width // COLS, unroll=True)
     def _(j):
         cols = pl.ds(pl.multiple_of(j * COLS, COLS), COLS)
         dnormed[:, cols] = nt(dpacked[...], wqkv_ref[cols, :]).astype(bf16)
@@ -461,7 +461,7 @@
     turn()
     gheld[0] = jnp.zeros((8, width), f32)
 
-    @pl.loop(0, windows)
+    @pl.loop(0, windows, unroll=2)
     def _(w):
         rows = pl.ds(pl.multiple_of(w * WCAP, WCAP), WCAP)
         dn = dnormed[rows, :].astype(f32)
@@ -476,24 +476,23 @@
         bg[rows, width:] = (xs[rows, width:].astype(f32) + dcentre).astype(bf16)
 
     gain_copy(0).start()
+    turn()
     collect_returns(1)
-    start_returns(1, (6, 5, 4, 3))
+    start_returns(1, (6, 5, 4, 3, 2, 1, 0))
+    advance_gain(0)
     turn()
-    advance_gain(0)
-    start_returns(1, (2, 1, 0))
     kept = (
         lax.broadcasted_iota(jnp.int32, (count, slots), 0) == wrow_ref[...]
     ).astype(f32).astype(bf16)
     for j in range(double // COLS):
         cols = slice(j * COLS, (j + 1) * COLS)
         own_ref[:, cols] = nn(kept, bg[:, cols]).astype(bf16)
-
     if not parts:
         for j in range(4 * width // COLS):
             grad_ref[:, j * COLS:(j + 1) * COLS] = gradient(j * COLS)
     for s in range(1, stages):
+        advance_gain(s)
         turn()
-        advance_gain(s)
 
     for h in range(2):
         for k in range(7):

time: 76.3 us -> 73.6 us (0.965)
  Pallas kernels: 75.4 us -> 72.8 us
    pallas_call x1, Pallas kernels: 72.7 us -> 70.1 us  [on_device(): pl.pallas_call(functools.partial(block_kernel, sizes, orders, bits, place...]
where the time goes in v5:
time: 73.6 us; the launch traced here: 73.4 us
  Pallas kernels  72.8 us (99%)
    pallas_call x1, Pallas kernels, on_device(): pl.pallas_call(functools.partial(block_kernel, sizes, orders, bits, place...  70.1 us
    pallas_call x1, Pallas kernels, on_device(): pl.pallas_call(functools.partial(finish_kernel, sizes), out_shape=tuple(f...  2.73 us

profile of v5, /device:TPU:0, one launch (start us, length us, event | category | flops | bytes accessed | tf_op | source)
XLA Modules:
  0.0 73.4 jit_solution(13460444717611537931)
XLA Ops:
  0.6 70.1 %block.1 = (bf16[256,1536]{1,0:T(8,128)(2,1)}, bf16[2,224,768]{2,1,0:T(8,128)(2,1)}, bf16[256,224]{1,0:T(8,128)(2,1)}, f32[8,768]{1,0:T(8,128)}, f32[24,2304]{1,0:T(8,128)}, /*index=5*/f32[24,768]{1,0:T(8,128)}) custom-call(bf16[256,768]{1,0:T(8,128)(2,1)} %refs_0_.1, bf16[256,768]{1,0:T(8,128)(2,1)} %refs_1_.1, s32[7,1,32]{2,1,0:T(1,128)} %bitcast.2, ...), custom_call_target="tpu_custom_call" | custom-call | tf_op jit(solution)/shard_map/block/pallas_call | solution.py:629
  70.7 2.7 %finish.1 = (bf16[256,768]{1,0:T(8,128)(2,1)}, bf16[256,768]{1,0:T(8,128)(2,1)}, f32[1,24]{1,0:T(1,128)}, f32[24,2304]{1,0:T(8,128)}, f32[24,768]{1,0:T(8,128)}) custom-call(bf16[256,1536]{1,0:T(8,128)(2,1)} %get-tuple-element.16.own_ref, bf16[2,224,768]{2,1,0:T(8,128)(2,1)} %get-tuple-element.17.back_ref, bf16[256,224]{1,0:T(8,128)(2,1)} %get-tuple-element.18.place_ref, ...), custom_call_target="tpu_custom_call" | custom-call | tf_op jit(solution)/shard_map/finish/pallas_call | solution.py:642
